TPU v7x, 32 devices: a whole 2x2x4 slice. The times are simulated.
32 devices in a mesh: snap: 2 (over y), brick: 16 (over z, x, core).
Axes of the slice: x: 2, y: 2, z: 4, core: 2. Of those that a mesh axis runs over, the one named last changes fastest.
Arguments:
- positions: float32 [2, 3, 4096], P('snap', None, 'brick'), may hold values from 0 to 7, as said below
- species: int32 [2, 4096], P('snap', 'brick'), may hold values from 0 to 4
- atom_words: int32 [2, 4096], P('snap', 'brick'), may hold values from 0 to 32767, as said below
- left_vector: float32 [2, 3, 4096], P('snap', None, 'brick'), may hold values from -6 to 6
- right_vector: float32 [5, 81, 80], replicated, may hold values from -0.006 to 0.006
- direction: float32 [5, 81, 80], replicated, may hold values from -6 to 6
- solution: float32 [5, 81, 80], replicated, may hold values from -6 to 6
- scalars: float32 [3], replicated, may hold values from 0.0005 to 2, as said below
Outputs:
- left_next: float32 [2, 3, 4096], P('snap', None, 'brick')
- right_next: float32 [5, 81, 80], replicated
- direction_next: float32 [5, 81, 80], replicated
- solution_next: float32 [5, 81, 80], replicated
- scalars_next: float32 [3], replicated
Inputs may be any that keep to these rules, and one draw needn't show every extreme that they name: `atom_words`: bit o-1 of atom g's word (o = 1..15) marks g+o as its neighbour; no bit points outside the snapshot. `positions`: rows 0 and 1 are transverse coordinates; row 2 is the offset along the column, below 0.2. `scalars`: alpha lies between 0.0005 and 0.002; rho_bar and phi_bar between 0.5 and 2.
All inputs are finite; a program needn't handle non-finite values.
Results may differ from a plain program's by a relative error of at most 0.0003.
Values sent between devices are 32-bit elements; how exact they have to be, the bound alone decides.
A program may use at most 64 MiB of HBM per device.

v0:
```python
import math

import jax
import jax.numpy as jnp
from jax import lax
from jax.sharding import PartitionSpec as P

SPECIES = 5
RADIAL = 16
WINDOW = 15
ITERS = 3


cutoff_sq = 36.0
spacing = 0.25
force_unit = 0.015625
tiny = 1e-06
HIGHEST = lax.Precision.HIGHEST


def with_halo(cells, sides, width):
    for axis, dim in sides:
        count = lax.axis_size(axis)
        ends = count - 1
        head = lax.slice_in_dim(cells, 0, width, axis=dim)
        tail = lax.slice_in_dim(cells, cells.shape[dim] - width, cells.shape[dim], axis=dim)
        cells = jnp.concatenate(
            [
                lax.ppermute(tail, axis, [(i, (i + 1) % count) for i in range(ends)]),
                cells,
                lax.ppermute(head, axis, [((i + 1) % count, i) for i in range(ends)]),
            ],
            axis=dim,
        )
    return cells


def window_offsets():
    return [shift_by for shift_by in range(1, WINDOW + 1)] + [
        -shift_by for shift_by in range(1, WINDOW + 1)
    ]


def radial_tables(scaled):
    envelope = jnp.maximum(1.0 - scaled, 0.0)
    argument = 2.0 * jnp.minimum(scaled, 1.0) - 1.0
    first_kind = [jnp.ones_like(argument), argument]
    second_kind = [jnp.ones_like(argument), 2.0 * argument]
    for degree in range(2, RADIAL):
        first_kind.append(2.0 * argument * first_kind[-1] - first_kind[-2])
        second_kind.append(2.0 * argument * second_kind[-1] - second_kind[-2])
    values = []
    slopes = []
    for degree in range(RADIAL):
        damping = 1.0 / (1.0 + degree)
        values.append(envelope * envelope * first_kind[degree] * damping)
        derivative = -2.0 * envelope * first_kind[degree]
        if degree > 0:
            derivative = derivative + 2.0 * degree * envelope * envelope * second_kind[degree - 1]
        slopes.append(derivative * damping)
    return (jnp.stack(values, axis=1), jnp.stack(slopes, axis=1))


def shifted_stack(padded, atom_count):
    return jnp.stack(
        [padded[:, WINDOW + offset : WINDOW + offset + atom_count] for offset in window_offsets()]
    )


def pair_tables(padded, atom_count):
    offsets = window_offsets()
    here = padded[:, WINDOW : WINDOW + atom_count]
    there = shifted_stack(padded, atom_count)
    lift = jnp.array([0.0, 0.0, 1.0], jnp.float32)
    steps_z = jnp.array(offsets, jnp.float32) * spacing
    delta = there[:, :3, :] - here[None, :3, :] + steps_z[:, None, None] * lift[None, :, None]
    scaled = jnp.sum(delta * delta, axis=1) / cutoff_sq
    radial, slope = radial_tables(scaled)
    kinds = jnp.arange(SPECIES, dtype=jnp.float32)
    other = (there[:, 3:4, :] == kinds[None, :, None]).astype(jnp.float32)
    here_words = here[4].astype(jnp.int32)
    there_words = there[:, 4, :].astype(jnp.int32)
    upward = jnp.array([offset > 0 for offset in offsets])
    source = jnp.where(upward[:, None], here_words[None, :], there_words)
    bits = jnp.array([offset - 1 if offset > 0 else -offset - 1 for offset in offsets], jnp.int32)
    linked = jnp.bitwise_and(jnp.right_shift(source, bits[:, None]), 1).astype(jnp.float32)
    return (delta, radial, slope, other, linked)


def density(padded, atom_count):
    delta, radial, slope, other, linked = pair_tables(padded, atom_count)
    grid = jnp.einsum("ozi,oni->zni", other, radial * linked[:, None, :], precision=HIGHEST)
    return grid.reshape(SPECIES * RADIAL, atom_count)


def slope_field(field_density, own_kinds, coefs):
    channels = field_density.shape[0]
    result = jnp.zeros_like(field_density)
    for kind in range(SPECIES):
        quad = coefs[kind, :channels, :]
        part = coefs[kind, channels][:, None] + jnp.dot(
            quad + quad.T, field_density, precision=HIGHEST
        ) / math.sqrt(channels)
        result = result + own_kinds[kind][None, :] * part
    return result


def pull_force(slopes, slopes_pad, padded, own_kinds, atom_count):
    delta, radial, slope, other, linked = pair_tables(padded, atom_count)
    own_grid = slopes.reshape(SPECIES, RADIAL, atom_count)
    there_slopes = shifted_stack(slopes_pad, atom_count).reshape(
        2 * WINDOW, SPECIES, RADIAL, atom_count
    )
    outward = jnp.einsum("ozi,zni->oni", other, own_grid, precision=HIGHEST)
    inward = jnp.einsum("zi,ozni->oni", own_kinds, there_slopes, precision=HIGHEST)
    strength = jnp.sum((outward + inward) * slope, axis=1) * linked * (2.0 / cutoff_sq)
    return jnp.sum(strength[:, None, :] * delta, axis=0)


def back_terms(field_density, values, value_pad, padded, own_kinds, atom_count):
    delta, radial, slope, other, linked = pair_tables(padded, atom_count)
    there_values = shifted_stack(value_pad, atom_count)
    project = jnp.sum(delta * (values[None] - there_values), axis=1) * linked * (2.0 / cutoff_sq)
    channels = field_density.shape[0]
    weights = jnp.einsum(
        "ozi,oni->zni", other, slope * project[:, None, :], precision=HIGHEST
    ).reshape(channels, atom_count)
    rows = []
    for kind in range(SPECIES):
        masked = field_density * own_kinds[kind][None, :]
        cross = jnp.dot(masked, weights.T, precision=HIGHEST)
        linear = jnp.sum(weights * own_kinds[kind][None, :], axis=1)
        rows.append(
            jnp.concatenate([(cross + cross.T) / math.sqrt(channels), linear[None, :]], axis=0)
        )
    return jnp.stack(rows)


def rotation(rho_bar, phi_bar, beta_norm, alpha_norm):
    rho_new = jnp.sqrt(rho_bar * rho_bar + beta_norm * beta_norm)
    cosine = rho_bar / rho_new
    sine_term = beta_norm / rho_new
    theta_term = sine_term * alpha_norm
    return (rho_new, theta_term, cosine * phi_bar, -cosine * alpha_norm, sine_term * phi_bar)


def shards(positions, species, atom_words, left_vector, right_vector, direction, solution, scalars):
    atom_count = positions.shape[2]
    coef_total = right_vector.size
    devices_all = lax.axis_size("snap") * lax.axis_size("brick")
    left_total = 3 * atom_count * positions.shape[0] * devices_all
    back_unit = force_unit * coef_total / left_total
    geometry = jnp.concatenate(
        [
            positions[0],
            species[0].astype(jnp.float32)[None],
            atom_words[0].astype(jnp.float32)[None],
        ],
        axis=0,
    )
    depth = WINDOW
    padded_all = with_halo(geometry, (("brick", 1),), depth)
    own_kinds = (species[0][None, :] == jnp.arange(SPECIES, dtype=jnp.int32)[:, None]).astype(
        jnp.float32
    )
    field_density = density(padded_all, atom_count)
    alpha_norm = scalars[0]
    rho_bar = scalars[1]
    phi_bar = scalars[2]
    left_now = left_vector[0]
    right_now = right_vector
    direction_now = direction
    solution_now = solution
    for sweep in range(ITERS):
        slopes = slope_field(field_density, own_kinds, right_now)
        slopes_pad = with_halo(slopes, (("brick", 1),), WINDOW)
        force = pull_force(slopes, slopes_pad, padded_all, own_kinds, atom_count)
        raw_left = force_unit * force - alpha_norm * left_now
        raw_pad = with_halo(raw_left, (("brick", 1),), WINDOW)
        local_terms = back_terms(
            field_density, raw_left, raw_pad, padded_all, own_kinds, atom_count
        )
        totals, squares = lax.psum((local_terms, jnp.sum(raw_left * raw_left)), ("snap", "brick"))
        beta_norm = jnp.sqrt(squares / left_total + tiny)
        left_now = raw_left / beta_norm
        right_raw = back_unit * totals / beta_norm - beta_norm * right_now
        alpha_norm = jnp.sqrt(jnp.sum(right_raw * right_raw) / coef_total + tiny)
        right_now = right_raw / alpha_norm
        rho_new, theta_term, phi_term, rho_bar, phi_bar = rotation(
            rho_bar, phi_bar, beta_norm, alpha_norm
        )
        solution_now = solution_now + phi_term / rho_new * direction_now
        direction_now = right_now - theta_term / rho_new * direction_now
    scalars_next = jnp.stack([alpha_norm, rho_bar, phi_bar])
    return (left_now[None], right_now, direction_now, solution_now, scalars_next)


def solution(mesh):
    placed = (
        P("snap", None, "brick"),
        P("snap", "brick"),
        P("snap", "brick"),
        P("snap", None, "brick"),
        P(),
        P(),
        P(),
        P(),
    )
    return jax.shard_map(
        shards,
        mesh=mesh,
        in_specs=placed,
        out_specs=(P("snap", None, "brick"), P(), P(), P(), P()),
        check_vma=False,
    )
```

profile of v0, /device:TPU:0, one launch (start us, length us, event | category | flops | bytes accessed | tf_op | source)
XLA Modules:
  0.0 622.0 jit_solution(14957779311237875102)
XLA Ops:
  10.6 3.0 collective-permute-start.1
  16.6 1.4 fusion.395
  23.7 2.6 multiply_multiply_fusion.19
  27.1 2.6 copy.5029
  29.8 3.4 convolution_bitcast_fusion.3
  36.9 5.3 collective-permute-start.3
  42.6 3.2 fusion.44
  46.0 2.8 copy.5070
  49.7 1.7 pad_maximum_fusion.5
  51.5 1.3 fusion.129
  58.0 4.3 collective-permute-start.5
  65.1 2.6 copy.5080
  67.8 5.3 broadcast_multiply_fusion
  73.0 1.4 copy.5081
  74.4 1.5 copy.5089
  76.9 1.4 fusion.153
  78.3 2.1 copy.5087
  82.2 1.4 fusion.154
  83.6 2.1 copy.5085
  87.5 1.4 fusion.155
  95.3 45.3 %psum.43 = f32[]{:T(128)} all-reduce(f32[]{:T(128)} %get-tuple-element.208), channel_id=1, replica_groups=mesh['snap'=2,'brick'=16] {'snap','brick'}, use_global_device_ids=true, to_apply=%region_14.15 | all-reduce | flops 1 | bytes 8 | tf_op jit(solution)/shard_map/psum | solution.py:183
  141.3 82.7 %all-reduce.4.cloned.1.call-done = f32[5,81,80]{2,1,0:T(8,128)} async-done(((f32[5,81,80]{2,1,0:T(8,128)}), f32[5,81,80]{2,1,0:T(8,128)}) %all-reduce.4.cloned.1.call-update) | async-done | bytes 129616 | tf_op jit(solution)/shard_map/psum | solution.py:183
  224.0 1.6 multiply_reduce_fusion.20
  229.6 2.8 collective-permute-start.7
  235.0 3.1 fusion.43
  238.1 2.0 copy.5098
  240.1 1.6 pad_maximum_fusion.3
  248.1 3.8 collective-permute-start.9
  255.6 2.4 copy.5107
  258.0 3.3 multiply_reduce_fusion.8
  261.3 1.4 copy.5108
  269.2 45.4 %psum.45 = f32[]{:T(128)} all-reduce(f32[]{:T(128)} %get-tuple-element.206), channel_id=1, replica_groups=mesh['snap'=2,'brick'=16] {'snap','brick'}, use_global_device_ids=true, to_apply=%region_27.28 | all-reduce | flops 1 | bytes 8 | tf_op jit(solution)/shard_map/psum | solution.py:183
  315.3 81.6 %all-reduce.6.cloned.1.call-done = f32[5,81,80]{2,1,0:T(8,128)} async-done(((f32[5,81,80]{2,1,0:T(8,128)}), f32[5,81,80]{2,1,0:T(8,128)}) %all-reduce.6.cloned.1.call-update) | async-done | bytes 129616 | tf_op jit(solution)/shard_map/psum | solution.py:183
  396.9 1.6 multiply_reduce_fusion.19
  402.5 3.4 collective-permute-start.11
  408.5 3.2 fusion.42
  411.7 2.0 copy.5120
  413.7 1.7 pad_maximum_fusion.1
  415.5 1.3 fusion.73
  417.0 1.6 pad_maximum_fusion
  418.7 1.3 fusion.59
  422.0 43.1 %psum.46 = f32[]{:T(128)} all-reduce(f32[]{:T(128)} %get-tuple-element.204), channel_id=1, replica_groups=mesh['snap'=2,'brick'=16] {'snap','brick'}, use_global_device_ids=true, to_apply=%region_33.34 | all-reduce | flops 1 | bytes 8 | tf_op jit(solution)/shard_map/psum | solution.py:183
  467.0 3.3 collective-permute-start.13
  474.6 2.4 copy.5129
  477.1 3.3 multiply_reduce_fusion.3
  480.4 1.5 copy.5130
  489.6 118.9 %all-reduce.8.cloned.1.call-done = f32[5,81,80]{2,1,0:T(8,128)} async-done(((f32[5,81,80]{2,1,0:T(8,128)}), f32[5,81,80]{2,1,0:T(8,128)}) %all-reduce.8.cloned.1.call-update) | async-done | bytes 129616 | tf_op jit(solution)/shard_map/psum | solution.py:183
  608.4 1.6 multiply_reduce_fusion.18
  (526 shorter events, 79.1 us)
Async XLA Ops:
  7.2 216.9 %all-reduce.4.cloned.1.call-start = ((), (), s32[]{:S(2)}) async-start(), calls=%async_computation | async-start | bytes 450560 | tf_op jit(solution)/shard_map/psum | solution.py:183
  9.3 9.7 %collective-permute-start = (f32[5,15]{1,0:T(8,128)S(1)}, f32[5,15]{1,0:T(8,128)S(1)}, u32[]{:S(2)}, u32[]{:S(2)}) collective-permute-start(f32[5,15]{1,0:T(8,128)S(1)} %get-tuple-element.400), channel_id=1, source_target_pairs={{1,0},{2,1},{3,2},{4,3},{5,4},{6,5},{7,6},{8,7},{9,8},{10,9},{11,1... | collective-permute-start | bytes 908 | tf_op jit(solution)/shard_map/ppermute | solution.py:31
  10.6 8.4 %collective-permute-start.1 = (f32[5,15]{1,0:T(8,128)S(1)}, f32[5,15]{1,0:T(8,128)S(1)}, u32[]{:S(2)}, u32[]{:S(2)}) collective-permute-start(f32[5,15]{1,0:T(8,128)S(1)} %get-tuple-element.399), channel_id=1, source_target_pairs={{0,1},{1,2},{2,3},{3,4},{4,5},{5,6},{6,7},{7,8},{8,9},{9,10},{10,1... | collective-permute-start | bytes 908 | tf_op jit(solution)/shard_map/ppermute | solution.py:29
  16.4 212.0 %copy-start.36 = (f32[1,256]{1,0:T(1,128)}, f32[1,256]{1,0:T(1,128)S(1)}, u32[]{:S(2)}) copy-start(f32[1,256]{1,0:T(1,128)S(1)} %get-tuple-element.398) | copy-start | bytes 3076
  29.7 3.8 copy-start.3
  35.6 14.1 %collective-permute-start.2 = (f32[80,15]{1,0:T(8,128)}, f32[80,15]{1,0:T(8,128)}, u32[]{:S(2)}, u32[]{:S(2)}) collective-permute-start(f32[80,15]{1,0:T(8,128)} %get-tuple-element.383), channel_id=1, source_target_pairs={{1,0},{2,1},{3,2},{4,3},{5,4},{6,5},{7,6},{8,7},{9,8},{10,9},{11,1... | collective-permute-start | bytes 14408 | tf_op jit(solution)/shard_map/ppermute | solution.py:31
  36.9 16.0 %collective-permute-start.3 = (f32[80,15]{1,0:T(8,128)}, f32[80,15]{1,0:T(8,128)S(1)}, u32[]{:S(2)}, u32[]{:S(2)}) collective-permute-start(f32[80,15]{1,0:T(8,128)} %get-tuple-element.382), channel_id=1, source_target_pairs={{0,1},{1,2},{2,3},{3,4},{4,5},{5,6},{6,7},{7,8},{8,9},{9,10},{10,1... | collective-permute-start | bytes 14408 | tf_op jit(solution)/shard_map/ppermute | solution.py:29
  42.6 6.2 copy-start.19
  42.6 6.2 copy-start.20
  45.9 3.0 copy-start.25
  45.9 3.0 copy-start.26
  45.9 3.0 copy-start.27
  45.9 3.0 copy-start.28
  45.9 3.0 copy-start.29
  45.9 3.0 copy-start.30
  45.9 3.0 copy-start.31
  45.9 3.0 copy-start.32
  45.9 3.0 copy-start.33
  56.1 6.2 collective-permute-start.4
  58.0 5.5 collective-permute-start.5
  74.4 14.4 %copy-start = (f32[5,16,256]{1,0,2:T(8,128)S(1)}, f32[5,16,256]{1,0,2:T(8,128)}, u32[]{:S(2)}) copy-start(f32[5,16,256]{1,0,2:T(8,128)} %get-tuple-element.222) | copy-start | bytes 245764
  76.0 15.0 %copy-start.6 = (f32[5,16,256]{2,1,0:T(8,128)}, f32[5,16,256]{2,1,0:T(8,128)S(1)}, u32[]{:S(2)}) copy-start(f32[5,16,256]{2,1,0:T(8,128)S(1)} %copy.5089) | copy-start | bytes 245764
  91.2 135.0 %copy-start.12 = (f32[5,16,256]{2,1,0:T(8,128)}, f32[5,16,256]{2,1,0:T(8,128)S(1)}, u32[]{:S(2)}) copy-start(f32[5,16,256]{2,1,0:T(8,128)S(1)} %copy.5030) | copy-start | bytes 245764
  95.1 301.9 %all-reduce.6.cloned.1.call-start = ((), (), s32[]{:S(2)}) async-start(), calls=%async_computation.1 | async-start | bytes 450560 | tf_op jit(solution)/shard_map/psum | solution.py:183
  229.6 13.7 %collective-permute-start.7 = (f32[80,15]{1,0:T(8,128)}, f32[80,15]{1,0:T(8,128)S(1)}, u32[]{:S(2)}, u32[]{:S(2)}) collective-permute-start(f32[80,15]{1,0:T(8,128)} %get-tuple-element.380), channel_id=1, source_target_pairs={{0,1},{1,2},{2,3},{3,4},{4,5},{5,6},{6,7},{7,8},{8,9},{9,10},{10,1... | collective-permute-start | bytes 14408 | tf_op jit(solution)/shard_map/ppermute | solution.py:29
  232.4 7.7 %collective-permute-start.6 = (f32[80,15]{1,0:T(8,128)S(1)}, f32[80,15]{1,0:T(8,128)}, u32[]{:S(2)}, u32[]{:S(2)}) collective-permute-start(f32[80,15]{1,0:T(8,128)S(1)} %get-tuple-element.381), channel_id=1, source_target_pairs={{1,0},{2,1},{3,2},{4,3},{5,4},{6,5},{7,6},{8,7},{9,8},{10,9},{11,1... | collective-permute-start | bytes 14408 | tf_op jit(solution)/shard_map/ppermute | solution.py:31
  244.2 10.4 %copy-start.41 = (pred[30]{0:T(512)(128)(4,1)S(1)}, pred[30]{0:T(512)(128)(4,1)}, u32[]{:S(2)}) copy-start(pred[30]{0:T(512)(128)(4,1)} %constant.161.clone) | copy-start | bytes 94
  245.1 12.8 %copy-start.37 = (f32[1,256]{1,0:T(1,128)S(1)}, f32[1,256]{1,0:T(1,128)}, u32[]{:S(2)}) copy-start(f32[1,256]{1,0:T(1,128)} %copy-done.36) | copy-start | bytes 3076
  246.2 5.7 collective-permute-start.8
  248.1 5.1 collective-permute-start.9
  258.0 4.8 copy-start.7
  265.2 136.1 %copy-start.38 = (f32[1,256]{1,0:T(1,128)S(1)}, f32[1,256]{1,0:T(1,128)}, u32[]{:S(2)}) copy-start(f32[1,256]{1,0:T(1,128)} %copy-done.36) | copy-start | bytes 3076
  269.1 339.3 %all-reduce.8.cloned.1.call-start = ((), (), s32[]{:S(2)}) async-start(), calls=%async_computation.2 | async-start | bytes 450560 | tf_op jit(solution)/shard_map/psum | solution.py:183
  401.8 5.4 copy-start.1
  402.5 14.5 %collective-permute-start.11 = (f32[80,15]{1,0:T(8,128)}, f32[80,15]{1,0:T(8,128)}, u32[]{:S(2)}, u32[]{:S(2)}) collective-permute-start(f32[80,15]{1,0:T(8,128)} %get-tuple-element.378), channel_id=1, source_target_pairs={{0,1},{1,2},{2,3},{3,4},{4,5},{5,6},{6,7},{7,8},{8,9},{9,10},{10,1... | collective-permute-start | bytes 14408 | tf_op jit(solution)/shard_map/ppermute | solution.py:29
  405.9 7.8 %collective-permute-start.10 = (f32[80,15]{1,0:T(8,128)}, f32[80,15]{1,0:T(8,128)}, u32[]{:S(2)}, u32[]{:S(2)}) collective-permute-start(f32[80,15]{1,0:T(8,128)} %get-tuple-element.379), channel_id=1, source_target_pairs={{1,0},{2,1},{3,2},{4,3},{5,4},{6,5},{7,6},{8,7},{9,8},{10,9},{11,1... | collective-permute-start | bytes 14408 | tf_op jit(solution)/shard_map/ppermute | solution.py:31
  408.5 5.2 copy-start.2
  420.9 56.1 %copy-start.39 = (f32[1,256]{1,0:T(1,128)S(1)}, f32[1,256]{1,0:T(1,128)}, u32[]{:S(2)}) copy-start(f32[1,256]{1,0:T(1,128)} %copy-done.36) | copy-start | bytes 3076
  465.7 5.2 collective-permute-start.12
  467.0 5.1 collective-permute-start.13
  477.0 4.9 copy-start.8
  477.0 5.1 copy-start.9
  477.0 5.3 copy-start.10
  477.0 5.5 copy-start.11
  477.0 5.8 copy-start.13
  480.4 5.7 copy-start.17
  480.4 5.9 copy-start.18
  480.4 8.6 %copy-start.46 = (f32[1,3,256]{2,1,0:T(4,128)S(1)}, f32[1,3,256]{2,1,0:T(4,128)}, u32[]{:S(2)}) copy-start(f32[1,3,256]{2,1,0:T(4,128)} %get-tuple-element.202) | copy-start | bytes 9220
  (16 other events, 25.0 us)
Sparse Core Ops, SparseCore 0:
  95.2 128.7 all-reduce.3
  269.2 127.6 all-reduce.5
  484.9 123.5 all-reduce.7
where the time goes:
time: 632 us; the launch traced here: 622 us
  waiting for transfers between devices  283 us (45%)
  blocking collectives  134 us (21%)
  local copies, waits for them, and re-layouts  54.4 us (9%)
  other arithmetic  52.8 us (8%)
  matrix products  38 us (6%)
  starting transfers between devices  35 us (6%)
  between operations  24.7 us (4%)
    psum x3, waiting for transfers between devices, shards(): lax.psum((local_terms, jnp.sum(raw_left * raw_left)), ('snap', 'brick'))  283 us
    psum x3, blocking collectives, shards(): lax.psum((local_terms, jnp.sum(raw_left * raw_left)), ('snap', 'brick'))  134 us
    ppermute x7, starting transfers between devices, with_halo(): lax.ppermute(tail, axis, [(i, (i + 1) % count) for i in range(ends)])  25.9 us
    concatenate x13, other arithmetic, with_halo(): jnp.concatenate([lax.ppermute(tail, axis, [(i, (i + 1) % count) for i in...  13.2 us
  transfers between devices with their start and end apart: 17, of which 3 were waited for; matrix products, arithmetic and copies ran while one was open for 7% of the time, Pallas kernels for 0%

commit v1 on v0

v1 whole, which is shorter than its diff:
```python
import functools
import math

import jax
import jax.numpy as jnp
from jax import lax
from jax.experimental import pallas as pl
from jax.experimental.pallas import tpu as pltpu
from jax.sharding import PartitionSpec as P

SPECIES = 5
RADIAL = 16
WINDOW = 15
ITERS = 3
CHANNELS = SPECIES * RADIAL
BLOCK = 88
HALF = CHANNELS // 2
ROWS = 256
LANES = 128
HALO = 64

cutoff_sq = 36.0
spacing = 0.25
force_unit = 0.015625
tiny = 1e-06
HIGHEST = lax.Precision.HIGHEST
MESH = pl.DeviceIdType.MESH


def turn(x, shift):
    width = x.shape[1]
    return pltpu.roll(x, shift % width, 1)


def row_sum(x):
    return jnp.sum(x, axis=0, keepdims=True)


def prepare(cells_ref, psi_ref, delta_ref, near_ref, masked_ref, own_ref, phi_ref, scaled_ref):
    width = cells_ref.shape[1]
    here = cells_ref[...]
    row_id = lax.broadcasted_iota(jnp.int32, (8, width), 0)
    near_ref[...] = jnp.full(near_ref.shape, -1.0, jnp.float32)
    scaled_ref[...] = jnp.ones(scaled_ref.shape, jnp.float32)
    for o in range(1, WINDOW + 1):
        there = turn(here, -o)
        delta = there - here + jnp.where(row_id == 2, spacing * o, 0.0)
        delta = jnp.where(row_id < 3, delta, 0.0)
        delta_ref[o - 1] = delta
        scaled_ref[o - 1 : o, :] = row_sum(delta * delta)
        near_ref[0, o - 1 : o, :] = there[3:4, :]
        near_ref[1, o - 1 : o, :] = turn(here, o)[3:4, :]
    scaled = scaled_ref[...] / cutoff_sq
    words = jnp.broadcast_to(here[4:5, :].astype(jnp.int32), scaled.shape)
    bits = lax.broadcasted_iota(jnp.int32, scaled.shape, 0)
    linked = jnp.bitwise_and(jnp.right_shift(words, bits), 1).astype(jnp.float32)
    envelope = jnp.maximum(1.0 - scaled, 0.0)
    argument = 2.0 * jnp.minimum(scaled, 1.0) - 1.0
    twice = 2.0 * argument
    square = envelope * envelope * linked
    line = -2.0 * envelope * linked
    first = [jnp.ones_like(argument), argument]
    second = [jnp.ones_like(argument), twice]
    for n in range(RADIAL):
        if n >= 2:
            first.append(twice * first[-1] - first[-2])
            second.append(twice * second[-1] - second[-2])
        damping = 1.0 / (1.0 + n)
        phi = square * first[n] * damping
        psi = line * first[n]
        if n > 0:
            psi = psi + 2.0 * n * square * second[n - 1]
        phi_ref[0, :, n, :] = phi
        psi_ref[0, :, n, :] = psi * damping
    for o in range(1, WINDOW + 1):
        phi_ref[1, o - 1] = turn(phi_ref[0, o - 1], o)
        psi_ref[1, o - 1] = turn(psi_ref[0, o - 1], o)
    kinds = here[3:4, :]
    own_ref[...] = jnp.where(
        jnp.broadcast_to(kinds, (8, width)) == row_id.astype(jnp.float32), 1.0, 0.0
    )
    for tile in range(width // LANES):
        at = slice(tile * LANES, (tile + 1) * LANES)
        sums = [jnp.zeros((RADIAL, LANES), jnp.float32) for _ in range(SPECIES)]
        for side in range(2):
            for o in range(WINDOW):
                value = phi_ref[side, o, :, at]
                kind = jnp.broadcast_to(near_ref[side, o : o + 1, at], (RADIAL, LANES))
                for c in range(SPECIES):
                    sums[c] = sums[c] + jnp.where(kind == c, value, 0.0)
        first_row = lax.broadcasted_iota(jnp.int32, (8, LANES), 0) == 0
        for z in range(SPECIES):
            own = own_ref[z : z + 1, at]
            for c in range(SPECIES):
                start = z * BLOCK + c * RADIAL
                masked_ref[start : start + RADIAL, at] = jnp.where(own > 0.5, sums[c], 0.0)
                if z == 0:
                    phi_ref[0, c, :, at] = sums[c]
            start = z * BLOCK + CHANNELS
            masked_ref[start : start + 8, at] = jnp.where(
                first_row, jnp.broadcast_to(own, (8, LANES)), 0.0
            )


def advance(total_ref, sums, state):
    v_in, pair_in, w_in, x_in, sc_in, raw_in = state
    left_total, coef_total = sums
    back_unit = force_unit * coef_total / left_total
    rho_bar = sc_in[1:2, 0:1]
    phi_bar = sc_in[2:3, 0:1]
    beta = jnp.sqrt(total_ref[ROWS - 8 : ROWS - 7, 0:1] / left_total + tiny)
    scale = back_unit / beta
    root = 1.0 / math.sqrt(CHANNELS)
    lane = lax.broadcasted_iota(jnp.int32, (HALF, LANES), 1)
    backs = []
    for z in range(SPECIES):
        packed = total_ref[z * HALF : (z + 1) * HALF, :]
        square = jnp.concatenate(
            [packed, jnp.zeros((LANES - HALF, LANES), jnp.float32)], axis=0
        )
        flipped = square.T[HALF:CHANNELS, :]
        lower = jnp.where(lane < HALF, flipped, turn(packed, -HALF))
        quad = jnp.concatenate([packed[:, :CHANNELS], lower[:, :CHANNELS]], axis=0) * root
        start = SPECIES * HALF + z
        backs.append((quad, total_ref[start : start + 1, :CHANNELS]))
    raws = []
    power = jnp.zeros((1, 1), jnp.float32)
    for z in range(SPECIES):
        quad = scale * backs[z][0] - beta * v_in[z, :CHANNELS, :]
        line = scale * backs[z][1] - beta * v_in[z, CHANNELS : CHANNELS + 1, :]
        raws.append((quad, line))
        power = power + jnp.sum(jnp.sum(quad * quad, axis=0, keepdims=True) + line * line,
                                axis=1, keepdims=True)
    alpha = jnp.sqrt(power / coef_total + tiny)
    rho = jnp.sqrt(rho_bar * rho_bar + beta * beta)
    cosine = rho_bar / rho
    sine = beta / rho
    theta = sine * alpha
    phi = cosine * phi_bar
    scalars = (alpha, -cosine * alpha, sine * phi_bar)
    inverse = 1.0 / alpha
    vs, pairs, ws, xs = [], [], [], []
    for z in range(SPECIES):
        quad = raws[z][0] * inverse
        line = raws[z][1] * inverse
        v = jnp.concatenate([quad, line], axis=0)
        w = w_in[z]
        vs.append(v)
        xs.append(x_in[z] + (phi / rho) * w)
        ws.append(v - (theta / rho) * w)
        old = pair_in[z * BLOCK : z * BLOCK + CHANNELS, :]
        pairs.append((2.0 * root * scale * backs[z][0] - beta * old) * inverse)
    left = raw_in[...] / beta
    return vs, pairs, ws, xs, scalars, left


def write_scalars(ref, scalars):
    row_id = lax.broadcasted_iota(jnp.int32, ref.shape, 0)
    ref[...] = jnp.where(row_id == 0, scalars[0], jnp.where(row_id == 1, scalars[1], scalars[2]))


def sweep(own_count, alpha, left, pair_ref, psi_ref, delta_ref, near_ref, masked_ref, own_ref,
          density, raw_ref, out_ref, slope_ref, pull_ref, weight_ref, rhs_ref, lhs_ref):
    width = masked_ref.shape[1]
    unit = 2.0 / cutoff_sq
    slope_ref[...] = lax.dot_general(
        pair_ref[...], masked_ref[...], (((0,), (0,)), ((), ())),
        precision=HIGHEST, preferred_element_type=jnp.float32,
    )
    for tile in range(width // LANES):
        at = slice(tile * LANES, (tile + 1) * LANES)
        parts = [slope_ref[c * RADIAL : (c + 1) * RADIAL, at] for c in range(SPECIES)]
        for side in range(2):
            for o in range(WINDOW):
                kind = jnp.broadcast_to(near_ref[side, o : o + 1, at], (RADIAL, LANES))
                chosen = parts[0]
                for c in range(1, SPECIES):
                    chosen = jnp.where(kind == c, parts[c], chosen)
                pull_ref[side, o : o + 1, at] = row_sum(chosen * psi_ref[side, o, :, at])
    force = jnp.zeros((8, width), jnp.float32)
    for o in range(1, WINDOW + 1):
        pull = pull_ref[0, o - 1 : o, :] + turn(pull_ref[1, o - 1 : o, :], -o)
        term = (unit * pull) * delta_ref[o - 1]
        force = force + term - turn(term, o)
    raw = force_unit * force - alpha * left
    raw_ref[...] = raw
    for o in range(1, WINDOW + 1):
        project = unit * row_sum(delta_ref[o - 1] * (raw - turn(raw, -o)))
        pull_ref[0, o - 1 : o, :] = project
        pull_ref[1, o - 1 : o, :] = turn(project, o)
    for tile in range(own_count // LANES):
        at = slice(tile * LANES, (tile + 1) * LANES)
        behind = slice(own_count + tile * LANES, own_count + (tile + 1) * LANES)
        sums = [jnp.zeros((RADIAL, LANES), jnp.float32) for _ in range(SPECIES)]
        for side in range(2):
            for o in range(WINDOW):
                value = psi_ref[side, o, :, at] * pull_ref[side, o : o + 1, at]
                kind = jnp.broadcast_to(near_ref[side, o : o + 1, at], (RADIAL, LANES))
                for c in range(SPECIES):
                    sums[c] = sums[c] + jnp.where(kind == c, value, 0.0)
        for c in range(SPECIES):
            rhs_ref[c * RADIAL : (c + 1) * RADIAL, at] = sums[c]
            rhs_ref[c * RADIAL : (c + 1) * RADIAL, behind] = density(c, at)
        rhs_ref[CHANNELS:, at] = jnp.zeros((LANES - CHANNELS, LANES), jnp.float32)
        rhs_ref[CHANNELS:, behind] = jnp.zeros((LANES - CHANNELS, LANES), jnp.float32)
        for z in range(SPECIES):
            own = own_ref[z : z + 1, at]
            for c in range(SPECIES):
                start = z * BLOCK + c * RADIAL
                lhs_ref[start : start + RADIAL, behind] = jnp.where(own > 0.5, sums[c], 0.0)
            start = z * BLOCK + CHANNELS
            lhs_ref[start : start + 8, behind] = jnp.zeros((8, LANES), jnp.float32)
        lhs_ref[:, at] = masked_ref[:, at]
    cross = lax.dot_general(
        lhs_ref[...], rhs_ref[...], (((1,), (1,)), ((), ())),
        precision=HIGHEST, preferred_element_type=jnp.float32,
    )
    lane = lax.broadcasted_iota(jnp.int32, (HALF, LANES), 1)
    out_ref[SPECIES * HALF :, :] = jnp.zeros((ROWS - SPECIES * HALF, LANES), jnp.float32)
    for z in range(SPECIES):
        upper = cross[z * BLOCK : z * BLOCK + HALF, :]
        lower = cross[z * BLOCK + HALF : z * BLOCK + CHANNELS, :]
        out_ref[z * HALF : (z + 1) * HALF, :] = jnp.where(lane < CHANNELS, upper, turn(lower, HALF))
        start = SPECIES * HALF + z
        out_ref[start : start + 1, :] = cross[z * BLOCK + CHANNELS : z * BLOCK + CHANNELS + 1, :]
    mine = raw[:, :own_count]
    square = jnp.sum(row_sum(mine * mine), axis=1, keepdims=True)
    out_ref[ROWS - 8 : ROWS, :] = jnp.broadcast_to(square, (8, LANES))


def first_kernel(own_count, cells_ref, sc_ref, pair_ref,
                 psi_ref, delta_ref, near_ref, masked_ref, own_ref, dens_ref, raw_ref, out_ref,
                 phi_ref, scaled_ref, *scratch):
    prepare(cells_ref, psi_ref, delta_ref, near_ref, masked_ref, own_ref, phi_ref, scaled_ref)
    dens_ref[...] = phi_ref[0, :SPECIES]
    cells = cells_ref[...]
    left = jnp.concatenate([cells[5:8], jnp.zeros((5, cells.shape[1]), jnp.float32)], axis=0)
    sweep(own_count, sc_ref[0:1, 0:1], left, pair_ref, psi_ref, delta_ref, near_ref, masked_ref,
          own_ref, lambda c, at: dens_ref[c, :, at], raw_ref, out_ref, *scratch)


def middle_kernel(own_count, sums, total_ref, v_in, pair_in, w_in, x_in, sc_in, raw_in,
                  psi_ref, delta_ref, near_ref, masked_ref, own_ref, dens_ref,
                  v_ref, pair_ref, w_ref, x_ref, sc_ref, raw_ref, out_ref, *scratch):
    vs, pairs, ws, xs, scalars, left = advance(
        total_ref, sums, (v_in, pair_in, w_in, x_in, sc_in, raw_in))
    for z in range(SPECIES):
        v_ref[z] = vs[z]
        w_ref[z] = ws[z]
        x_ref[z] = xs[z]
        start = z * BLOCK
        pair_ref[start : start + CHANNELS, :] = pairs[z]
        pair_ref[start + CHANNELS : start + BLOCK, :] = jnp.zeros(
            (BLOCK - CHANNELS, CHANNELS), jnp.float32)
        pair_ref[start + CHANNELS : start + CHANNELS + 1, :] = vs[z][CHANNELS:]
    write_scalars(sc_ref, scalars)
    sweep(own_count, scalars[0], left, pair_ref, psi_ref, delta_ref, near_ref, masked_ref,
          own_ref, lambda c, at: dens_ref[c, :, at], raw_ref, out_ref, *scratch)


def last_kernel(sums, total_ref, v_in, pair_in, w_in, x_in, sc_in, raw_in,
                v_ref, w_ref, x_ref, sc_ref, left_ref):
    vs, _, ws, xs, scalars, left = advance(
        total_ref, sums, (v_in, pair_in, w_in, x_in, sc_in, raw_in))
    for z in range(SPECIES):
        v_ref[z] = vs[z]
        w_ref[z] = ws[z]
        x_ref[z] = xs[z]
    write_scalars(sc_ref, scalars)
    left_ref[...] = left[0:3, : left_ref.shape[1]]


def reduce_kernel(n_snap, n_brick, x_ref, o_ref, slots, full, send_a, recv_a, send_b, recv_b):
    count = n_snap * n_brick
    owners = min(count, ROWS // 8)
    stride = count // owners
    rows = ROWS // owners
    me = lax.axis_index("snap") * n_brick + lax.axis_index("brick")
    barrier = pltpu.get_barrier_semaphore()

    def device(p):
        return (p // n_brick, lax.rem(p, n_brick))

    def every_owner(act):
        if stride == 1:
            def body(k, carry):
                act(lax.rem(me + k, count))
                return carry
            lax.fori_loop(1, count, body, 0)
        else:
            def body(k, carry):
                p = lax.rem(me // stride + k, owners) * stride

                @pl.when(p != me)
                def _():
                    act(p)
                return carry
            lax.fori_loop(0, owners, body, 0)

    def everyone(act):
        def body(k, carry):
            act(lax.rem(me + k, count))
            return carry
        lax.fori_loop(1, count, body, 0)

    def when_owner(yes, no):
        if stride == 1:
            yes()
        else:
            pl.when(lax.rem(me, stride) == 0)(yes)
            pl.when(lax.rem(me, stride) != 0)(no)

    def greet(p):
        pl.semaphore_signal(barrier, inc=1, device_id=device(p), device_id_type=MESH)

    def greet_all():
        everyone(greet)
        pl.semaphore_wait(barrier, count - 1)

    def greet_owners():
        every_owner(greet)
        pl.semaphore_wait(barrier, owners)

    when_owner(greet_all, greet_owners)

    def chunk(ref, p):
        return ref.at[pl.ds(pl.multiple_of((p // stride) * rows, rows), rows), :]

    def send_part(p):
        pltpu.make_async_remote_copy(
            src_ref=chunk(x_ref, p), dst_ref=slots.at[me], send_sem=send_a, recv_sem=recv_a,
            device_id=device(p), device_id_type=MESH,
        ).start()

    def bytes_of(amount, sem):
        view = full.at[pl.ds(0, amount * rows), :]
        pltpu.make_async_copy(view, view, sem).wait()

    def gather_slots(amount, sem):
        view = slots.at[pl.ds(0, amount)]
        pltpu.make_async_copy(view, view, sem).wait()

    every_owner(send_part)

    def finish_owner():
        mine = pl.multiple_of((me // stride) * rows, rows)
        slots[me] = x_ref[pl.ds(mine, rows), :]
        gather_slots(count - 1, recv_a)
        total = slots[0]
        for p in range(1, count):
            total = total + slots[p]
        full[pl.ds(mine, rows), :] = total

        def send_sum(p):
            pltpu.make_async_remote_copy(
                src_ref=chunk(full, me), dst_ref=chunk(full, me), send_sem=send_b,
                recv_sem=recv_b, device_id=device(p), device_id_type=MESH,
            ).start()

        everyone(send_sum)
        bytes_of(owners - 1, send_a)
        bytes_of(owners - 1, recv_b)
        gather_slots(count - 1, send_b)

    def finish_other():
        bytes_of(owners, send_a)
        bytes_of(owners, recv_b)

    when_owner(finish_owner, finish_other)
    o_ref[...] = full[...]


def shards(n_snap, n_brick, positions, species, atom_words, left_vector, right_vector, direction,
           solution_in, scalars):
    own_count = positions.shape[2]
    width = own_count + 2 * HALO
    coef_total = float(right_vector.size)
    left_total = float(3 * own_count * n_snap * n_brick * positions.shape[0])
    sums = (left_total, coef_total)
    f32 = jnp.float32

    own = jnp.concatenate(
        [positions[0], species.astype(f32), atom_words.astype(f32), left_vector[0]], axis=0)
    right = lax.ppermute(own[:, :HALO], "brick", [(i + 1, i) for i in range(n_brick - 1)])
    left = lax.ppermute(own[:, -HALO:], "brick", [(i, i + 1) for i in range(n_brick - 1)])
    cells = jnp.concatenate([own, right, left], axis=1)

    quad = right_vector[:, :CHANNELS, :]
    pair = (quad + jnp.swapaxes(quad, 1, 2)) / math.sqrt(CHANNELS)
    pair = jnp.concatenate(
        [pair, right_vector[:, CHANNELS:, :],
         jnp.zeros((SPECIES, BLOCK - CHANNELS - 1, CHANNELS), f32)], axis=1
    ).reshape(SPECIES * BLOCK, CHANNELS)
    sc = jnp.broadcast_to(jnp.pad(scalars, (0, 5))[:, None], (8, LANES))

    def shape(*dims):
        return jax.ShapeDtypeStruct(dims, f32)

    vmem = pl.BlockSpec(memory_space=pltpu.VMEM)
    params = pltpu.CompilerParams(vmem_limit_bytes=32 * 2**20)
    tables = [
        shape(2, 16, RADIAL, width), shape(16, 8, width), shape(2, 16, width),
        shape(SPECIES * BLOCK, width), shape(8, width), shape(SPECIES, RADIAL, width),
    ]
    coefs = shape(SPECIES, CHANNELS + 1, CHANNELS)
    pairs = shape(SPECIES * BLOCK, CHANNELS)
    raws = shape(8, width)
    message = shape(ROWS, LANES)
    work = [
        pltpu.VMEM((CHANNELS, width), f32), pltpu.VMEM((2, 16, width), f32),
        pltpu.VMEM((8, LANES), f32), pltpu.VMEM((LANES, 2 * own_count), f32),
        pltpu.VMEM((SPECIES * BLOCK, 2 * own_count), f32),
    ]

    def call(body, inputs, outs, scratch):
        return pl.pallas_call(
            body, out_shape=outs, in_specs=[vmem] * len(inputs), out_specs=[vmem] * len(outs),
            scratch_shapes=scratch, compiler_params=params,
        )(*inputs)

    count = n_snap * n_brick
    owners = min(count, ROWS // 8)

    def total(part):
        return pl.pallas_call(
            functools.partial(reduce_kernel, n_snap, n_brick),
            out_shape=message, in_specs=[vmem], out_specs=vmem,
            scratch_shapes=[
                pltpu.VMEM((count, ROWS // owners, LANES), f32), pltpu.VMEM((ROWS, LANES), f32),
            ] + [pltpu.SemaphoreType.DMA] * 4,
            compiler_params=pltpu.CompilerParams(collective_id=0, has_side_effects=True),
        )(part)

    *kept, raw, part = call(
        functools.partial(first_kernel, own_count), [cells, sc, pair], tables + [raws, message],
        [pltpu.VMEM((2, 16, RADIAL, width), f32), pltpu.VMEM((16, width), f32)] + work)
    v, w, x = right_vector, direction, solution_in
    for _ in range(ITERS - 1):
        v, pair, w, x, sc, raw, part = call(
            functools.partial(middle_kernel, own_count, sums),
            [total(part), v, pair, w, x, sc, raw] + kept,
            [coefs, pairs, coefs, coefs, shape(8, LANES), raws, message], work)
    v, w, x, sc, left_next = call(
        functools.partial(last_kernel, sums), [total(part), v, pair, w, x, sc, raw],
        [coefs, coefs, coefs, shape(8, LANES), shape(3, own_count)], [])
    return (left_next[None], v, w, x, sc[:3, 0])


def solution(mesh):
    placed = (
        P("snap", None, "brick"), P("snap", "brick"), P("snap", "brick"),
        P("snap", None, "brick"), P(), P(), P(), P(),
    )
    return jax.shard_map(
        functools.partial(shards, mesh.shape["snap"], mesh.shape["brick"]),
        mesh=mesh, in_specs=placed,
        out_specs=(P("snap", None, "brick"), P(), P(), P(), P()), check_vma=False,
    )
```

time: 632 us -> 81.3 us (0.13); the launches traced: 622 us -> 80.8 us
  waiting for transfers between devices: 283 us -> 0.01 us
  blocking collectives: 134 us -> 0 us
  Pallas kernels: 0 us -> 59.5 us
  other arithmetic: 52.8 us -> 1.61 us
  local copies, waits for them, and re-layouts: 54.4 us -> 14.4 us
  matrix products: 38 us -> 0 us
  starting transfers between devices: 35 us -> 4.44 us
  between operations: 24.7 us -> 0.84 us
    psum x3 -> x0, waiting for transfers between devices: 283 us -> none  [shards(): lax.psum((local_terms, jnp.sum(raw_left * raw_left)), ('snap', 'brick'))]
    psum x3 -> x0, blocking collectives: 134 us -> none  [shards(): lax.psum((local_terms, jnp.sum(raw_left * raw_left)), ('snap', 'brick'))]
    pallas_call x0 -> x7, Pallas kernels: none -> 59.5 us  [the longest x3 50.5 us: total(): pl.pallas_call(functools.partial(reduce_kernel, n_snap, n_brick), out_sha...]
    dot_general x37 -> x0, matrix products: 38 us -> none  [the longest x3 11.9 us: back_terms(): jnp.einsum('ozi,oni->zni', other, slope * project[:, None, :], precision=...]
    ppermute x14 -> x2, starting transfers between devices: 34.9 us -> 4.44 us  [the longest x1 3.16 us: shards(): lax.ppermute(own[:, -HALO:], 'brick', [(i, i + 1) for i in range(n_brick...]
    mul x16 -> x0, local copies, waits for them, and re-layouts: 16.8 us -> none  [the longest x6 7.4 us: back_terms(): slope * project[:, None, :]]
    concatenate x14 -> x3, other arithmetic: 13.2 us -> 0.21 us  [the longest x1 0.12 us: shards(): jnp.concatenate([pair, right_vector[:, CHANNELS:, :], jnp.zeros((SPECIES,...]
    dot_general x18 -> x0, local copies, waits for them, and re-layouts: 9.83 us -> none  [the longest x3 6.79 us: pull_force(): outward = jnp.einsum('ozi,zni->oni', other, own_grid, precision=HIGHEST)]
  transfers between devices with their start and end apart: 17 -> 2, of which waited for: 3 -> 0; matrix products, arithmetic and copies ran while one was open for 7% -> 2% of each run, Pallas kernels for 0% -> 0%
where the time goes in v1:
time: 81.3 us; the launch traced here: 80.8 us
  Pallas kernels  59.5 us (73%)
  local copies, waits for them, and re-layouts  14.4 us (18%)
  starting transfers between devices  4.44 us (5%)
  other arithmetic  1.61 us (2%)
  between operations  0.84 us (1%)
    pallas_call x3, Pallas kernels, total(): pl.pallas_call(functools.partial(reduce_kernel, n_snap, n_brick), out_sha...  50.5 us
    unnamed x38, local copies, waits for them, and re-layouts  12.3 us
    pallas_call x4, Pallas kernels, call(): pl.pallas_call(body, out_shape=outs, in_specs=[vmem] * len(inputs), out_s...  9.05 us
    ppermute x1, starting transfers between devices, shards(): lax.ppermute(own[:, -HALO:], 'brick', [(i, i + 1) for i in range(n_brick...  3.16 us
  transfers between devices with their start and end apart: 2, of which 0 were waited for; matrix products, arithmetic and copies ran while one was open for 2% of the time, Pallas kernels for 0%

profile of v1, /device:TPU:0, one launch (start us, length us, event | category | flops | bytes accessed | tf_op | source)
XLA Modules:
  0.0 80.8 jit_solution(13887305309234520858)
XLA Ops:
  0.6 0.0 copy-start.13
  0.6 0.7 convert_element_type.8
  1.3 0.7 convert_element_type.9
  2.0 0.0 copy-done.13
  2.0 0.7 copy_bitcast_fusion
  2.7 0.1 fusion.1
  2.8 1.3 %collective-permute-start = (f32[8,64]{1,0:T(8,128)S(1)}, f32[8,64]{1,0:T(8,128)S(1)}, u32[]{:S(2)}, u32[]{:S(2)}) collective-permute-start(f32[8,64]{1,0:T(8,128)S(1)} %get-tuple-element.69), channel_id=1, source_target_pairs={{1,0},{2,1},{3,2},{4,3},{5,4},{6,5},{7,6},{8,7},{9,8},{10,9},{11,1... | collective-permute-start | bytes 6152 | tf_op jit(solution)/shard_map/ppermute | solution.py:384
  4.1 0.0 copy-start.10
  4.1 3.2 %collective-permute-start.1 = (f32[8,64]{1,0:T(8,128)S(1)}, f32[8,64]{1,0:T(8,128)S(1)}, u32[]{:S(2)}, u32[]{:S(2)}) collective-permute-start(f32[8,64]{1,0:T(8,128)S(1)} %get-tuple-element.70), channel_id=1, source_target_pairs={{0,1},{1,2},{2,3},{3,4},{4,5},{5,6},{6,7},{7,8},{8,9},{9,10},{10,1... | collective-permute-start | bytes 6152 | tf_op jit(solution)/shard_map/ppermute | solution.py:385
  7.3 1.0 %slice.18 = f32[5,1,80]{1,2,0:T(8,128)S(1)} slice(f32[5,81,80]{1,2,0:T(8,128)} %param.12), slice={[0:5], [80:81], [0:80]} | slice | bytes 3200 | tf_op jit(solution)/shard_map/slice | solution.py:391
  8.3 0.0 copy-done.10
  8.3 0.1 copy.22
  8.5 0.1 pad.7.clone
  8.6 0.1 maximum_maximum_fusion
  8.7 0.0 copy-start.14
  8.7 0.1 copy.24.v_in
  8.9 0.5 copy-done.14
  9.4 0.1 copy.23
  9.5 0.8 copy-done.11
  10.3 0.1 copy.25.w_in
  10.4 0.8 copy-done.12
  11.2 0.1 copy.26.x_in
  11.4 0.0 collective-permute-done
  11.4 0.0 collective-permute-done.1
  11.4 0.1 pad_maximum_fusion.cells_ref
  11.5 0.1 broadcast_in_dim.12.sc_ref.sc_in
  11.5 3.3 %shard_map.119 = (f32[2,16,16,384]{3,2,1,0:T(8,128)S(1)}, f32[16,8,384]{2,1,0:T(8,128)S(1)}, f32[2,16,384]{2,1,0:T(8,128)S(1)}, f32[440,384]{1,0:T(8,128)S(1)}, ...) custom-call(f32[8,384]{1,0:T(8,128)S(1)} %pad_maximum_fusion.cells_ref, ...), custom_call_target="tpu_custom_call" | custom-call | tf_op jit(solution)/shard_map/pallas_call | solution.py:416
  14.8 0.7 copy-done.9
  15.5 19.6 %shard_map.120.total_ref = f32[256,128]{1,0:T(8,128)} custom-call(f32[256,128]{1,0:T(8,128)} %copy-done.9), custom_call_target="tpu_custom_call" | custom-call | tf_op jit(solution)/shard_map/pallas_call | solution.py:425
  35.1 0.0 copy-start.1
  35.1 0.9 %copy-done.1 = f32[256,128]{1,0:T(8,128)S(1)} copy-done((f32[256,128]{1,0:T(8,128)S(1)}, f32[256,128]{1,0:T(8,128)}, u32[]{:S(2)}) %copy-start.1) | copy-done | bytes 131096
  36.0 2.7 %shard_map.121 = (f32[5,81,80]{2,1,0:T(8,128)S(1)}, f32[440,80]{1,0:T(8,128)S(1)}, f32[5,81,80]{2,1,0:T(8,128)S(1)}, f32[5,81,80]{2,1,0:T(8,128)S(1)}, f32[8,128...) custom-call(f32[256,128]{1,0:T(8,128)S(1)} %copy-done.1, f32[5,81,80]{2,1,0:T(8,128)S(1)} %copy.24.v_in, ...), custom_call_target="tpu_custom_call" | custom-call | tf_op jit(solution)/shard_map/pallas_call | solution.py:416
  38.7 0.7 copy-done.3
  39.3 0.7 copy-done.8
  40.0 15.2 %shard_map.122.total_ref = f32[256,128]{1,0:T(8,128)} custom-call(f32[256,128]{1,0:T(8,128)} %copy-done.8), custom_call_target="tpu_custom_call" | custom-call | tf_op jit(solution)/shard_map/pallas_call | solution.py:425
  55.2 0.0 copy-done.4
  55.2 0.9 %copy-done = f32[256,128]{1,0:T(8,128)S(1)} copy-done((f32[256,128]{1,0:T(8,128)S(1)}, f32[256,128]{1,0:T(8,128)}, u32[]{:S(2)}) %copy-start) | copy-done | bytes 131096
  56.1 2.7 %shard_map.123 = (f32[5,81,80]{2,1,0:T(8,128)S(1)}, f32[440,80]{1,0:T(8,128)S(1)}, f32[5,81,80]{2,1,0:T(8,128)S(1)}, f32[5,81,80]{2,1,0:T(8,128)S(1)}, f32[8,128...) custom-call(f32[256,128]{1,0:T(8,128)S(1)} %copy-done, f32[5,81,80]{2,1,0:T(8,128)S(1)} %get-tuple-element.41.v_in, ...), custom_call_target="tpu_custom_call" | custom-call | tf_op jit(solution)/shard_map/pallas_call | solution.py:416
  58.8 0.7 copy-done.5
  59.5 0.7 copy-done.7
  60.2 15.7 %shard_map.124.total_ref = f32[256,128]{1,0:T(8,128)} custom-call(f32[256,128]{1,0:T(8,128)} %copy-done.7), custom_call_target="tpu_custom_call" | custom-call | tf_op jit(solution)/shard_map/pallas_call | solution.py:425
  75.9 0.9 %copy-done.2 = f32[256,128]{1,0:T(8,128)S(1)} copy-done((f32[256,128]{1,0:T(8,128)S(1)}, f32[256,128]{1,0:T(8,128)}, u32[]{:S(2)}) %copy-start.2) | copy-done | bytes 131096
  76.8 0.4 shard_map.125
  77.2 0.6 copy.27
  77.7 0.6 slice_reduce_fusion
  78.4 0.8 %copy.28 = f32[5,81,80]{1,2,0:T(8,128)} copy(f32[5,81,80]{2,1,0:T(8,128)S(1)} %get-tuple-element.65) | data formatting | bytes 259200
  79.2 0.8 %copy.29 = f32[5,81,80]{1,2,0:T(8,128)} copy(f32[5,81,80]{2,1,0:T(8,128)S(1)} %get-tuple-element.66) | data formatting | bytes 259200
  80.0 0.8 %copy.30 = f32[5,81,80]{1,2,0:T(8,128)} copy(f32[5,81,80]{2,1,0:T(8,128)S(1)} %get-tuple-element.67) | data formatting | bytes 259200
  (16 shorter events, 0.1 us)
Async XLA Ops:
  0.6 1.4 %copy-start.13 = (f32[1,3,256]{2,0,1:T(1,128)S(1)}, f32[1,3,256]{2,0,1:T(1,128)}, u32[]{:S(2)}) copy-start(f32[1,3,256]{2,0,1:T(1,128)} %param.11) | copy-start | bytes 9220
  2.8 8.6 %collective-permute-start = (f32[8,64]{1,0:T(8,128)S(1)}, f32[8,64]{1,0:T(8,128)S(1)}, u32[]{:S(2)}, u32[]{:S(2)}) collective-permute-start(f32[8,64]{1,0:T(8,128)S(1)} %get-tuple-element.69), channel_id=1, source_target_pairs={{1,0},{2,1},{3,2},{4,3},{5,4},{6,5},{7,6},{8,7},{9,8},{10,9},{11,1... | collective-permute-start | bytes 6152 | tf_op jit(solution)/shard_map/ppermute | solution.py:384
  4.1 4.2 %copy-start.10 = (f32[5,81,80]{1,2,0:T(8,128)S(1)}, f32[5,81,80]{1,2,0:T(8,128)}, u32[]{:S(2)}) copy-start(f32[5,81,80]{1,2,0:T(8,128)} %param.12) | copy-start | bytes 388804
  4.1 7.3 %collective-permute-start.1 = (f32[8,64]{1,0:T(8,128)S(1)}, f32[8,64]{1,0:T(8,128)S(1)}, u32[]{:S(2)}, u32[]{:S(2)}) collective-permute-start(f32[8,64]{1,0:T(8,128)S(1)} %get-tuple-element.70), channel_id=1, source_target_pairs={{0,1},{1,2},{2,3},{3,4},{4,5},{5,6},{6,7},{7,8},{8,9},{9,10},{10,1... | collective-permute-start | bytes 6152 | tf_op jit(solution)/shard_map/ppermute | solution.py:385
  8.7 0.7 copy-start.14
  9.4 0.9 %copy-start.11 = (f32[5,81,80]{1,2,0:T(8,128)S(1)}, f32[5,81,80]{1,2,0:T(8,128)}, u32[]{:S(2)}) copy-start(f32[5,81,80]{1,2,0:T(8,128)} %param.13) | copy-start | bytes 388804
  10.3 0.9 %copy-start.12 = (f32[5,81,80]{1,2,0:T(8,128)S(1)}, f32[5,81,80]{1,2,0:T(8,128)}, u32[]{:S(2)}) copy-start(f32[5,81,80]{1,2,0:T(8,128)} %param.14) | copy-start | bytes 388804
  14.8 0.7 copy-start.9
  35.1 0.9 %copy-start.1 = (f32[256,128]{1,0:T(8,128)S(1)}, f32[256,128]{1,0:T(8,128)}, u32[]{:S(2)}) copy-start(f32[256,128]{1,0:T(8,128)} %shard_map.120.total_ref) | copy-start | bytes 393220
  38.7 0.7 copy-start.3
  39.3 0.7 copy-start.8
  40.0 15.2 %copy-start.4 = (f32[5,81,80]{2,1,0:T(8,128)S(1)}, f32[5,81,80]{2,1,0:T(8,128)}, u32[]{:S(2)}) copy-start(f32[5,81,80]{2,1,0:T(8,128)} %copy-done.3) | copy-start | bytes 388804
  55.2 0.9 %copy-start = (f32[256,128]{1,0:T(8,128)S(1)}, f32[256,128]{1,0:T(8,128)}, u32[]{:S(2)}) copy-start(f32[256,128]{1,0:T(8,128)} %shard_map.122.total_ref) | copy-start | bytes 393220
  58.8 0.7 copy-start.5
  59.5 0.7 copy-start.7
  60.2 15.7 %copy-start.6 = (f32[5,81,80]{2,1,0:T(8,128)S(1)}, f32[5,81,80]{2,1,0:T(8,128)}, u32[]{:S(2)}) copy-start(f32[5,81,80]{2,1,0:T(8,128)} %copy-done.5) | copy-start | bytes 388804
  75.9 0.9 %copy-start.2 = (f32[256,128]{1,0:T(8,128)S(1)}, f32[256,128]{1,0:T(8,128)}, u32[]{:S(2)}) copy-start(f32[256,128]{1,0:T(8,128)} %shard_map.124.total_ref) | copy-start | bytes 393220

commit v2 on v1

v2 whole, which is shorter than its diff:
```python
import functools
import math

import jax
import jax.numpy as jnp
from jax import lax
from jax.experimental import pallas as pl
from jax.experimental.pallas import tpu as pltpu
from jax.sharding import PartitionSpec as P

SPECIES = 5
RADIAL = 16
WINDOW = 15
ITERS = 3
CHANNELS = SPECIES * RADIAL
BLOCK = 128
HALF = CHANNELS // 2
TERMS = CHANNELS + 1
MOVE = 128 - TERMS
ROWS = 256
LANES = 128
HALO = 64

cutoff_sq = 36.0
spacing = 0.25
force_unit = 0.015625
tiny = 1e-06
HIGHEST = lax.Precision.HIGHEST
MESH = pl.DeviceIdType.MESH


def turn(x, shift):
    width = x.shape[1]
    return pltpu.roll(x, shift % width, 1)


def row_sum(x):
    return jnp.sum(x, axis=0, keepdims=True)


def prepare(cells_ref, psi_ref, delta_ref, near_ref, masked_ref, own_ref, dens_ref, phi_ref,
            scaled_ref):
    width = cells_ref.shape[1]
    here = cells_ref[...]
    row_id = lax.broadcasted_iota(jnp.int32, (8, width), 0)
    near_ref[...] = jnp.full(near_ref.shape, -1.0, jnp.float32)
    scaled_ref[...] = jnp.ones(scaled_ref.shape, jnp.float32)
    for o in range(1, WINDOW + 1):
        there = turn(here, -o)
        delta = there - here + jnp.where(row_id == 2, spacing * o, 0.0)
        delta = jnp.where(row_id < 3, delta, 0.0)
        delta_ref[o - 1] = delta
        scaled_ref[o - 1 : o, :] = row_sum(delta * delta)
        near_ref[0, o - 1 : o, :] = there[3:4, :]
        near_ref[1, o - 1 : o, :] = turn(here, o)[3:4, :]
    scaled = scaled_ref[...] / cutoff_sq
    words = jnp.broadcast_to(here[4:5, :].astype(jnp.int32), scaled.shape)
    bits = lax.broadcasted_iota(jnp.int32, scaled.shape, 0)
    linked = jnp.bitwise_and(jnp.right_shift(words, bits), 1).astype(jnp.float32)
    envelope = jnp.maximum(1.0 - scaled, 0.0)
    argument = 2.0 * jnp.minimum(scaled, 1.0) - 1.0
    twice = 2.0 * argument
    square = envelope * envelope * linked
    line = -2.0 * envelope * linked
    first = [jnp.ones_like(argument), argument]
    second = [jnp.ones_like(argument), twice]
    for n in range(RADIAL):
        if n >= 2:
            first.append(twice * first[-1] - first[-2])
            second.append(twice * second[-1] - second[-2])
        damping = 1.0 / (1.0 + n)
        phi = square * first[n] * damping
        psi = line * first[n]
        if n > 0:
            psi = psi + 2.0 * n * square * second[n - 1]
        phi_ref[0, :, n, :] = phi
        psi_ref[0, :, n, :] = psi * damping
    for o in range(1, WINDOW + 1):
        phi_ref[1, o - 1] = turn(phi_ref[0, o - 1], o)
        psi_ref[1, o - 1] = turn(psi_ref[0, o - 1], o)
    kinds = here[3:4, :]
    own_ref[...] = jnp.where(
        jnp.broadcast_to(kinds, (8, width)) == row_id.astype(jnp.float32), 1.0, 0.0
    )
    masked_ref[...] = jnp.zeros(masked_ref.shape, jnp.float32)
    for tile in range(width // LANES):
        at = slice(tile * LANES, (tile + 1) * LANES)
        sums = [jnp.zeros((RADIAL, LANES), jnp.float32) for _ in range(SPECIES)]
        for side in range(2):
            for o in range(WINDOW):
                value = phi_ref[side, o, :, at]
                kind = jnp.broadcast_to(near_ref[side, o : o + 1, at], (RADIAL, LANES))
                for c in range(SPECIES):
                    sums[c] = sums[c] + jnp.where(kind == c, value, 0.0)
        first_row = lax.broadcasted_iota(jnp.int32, (8, LANES), 0) == 0
        for z in range(SPECIES):
            own = own_ref[z : z + 1, at]
            for c in range(SPECIES):
                start = z * BLOCK + c * RADIAL
                masked_ref[start : start + RADIAL, at] = jnp.where(own > 0.5, sums[c], 0.0)
                if z == 0:
                    dens_ref[c * RADIAL : (c + 1) * RADIAL, at] = sums[c]
            start = z * BLOCK + CHANNELS
            masked_ref[start : start + 8, at] = jnp.where(
                first_row, jnp.broadcast_to(own, (8, LANES)), 0.0
            )


def advance(total, sums, v_ref, w_ref, x_ref, pair_ref, sc_ref, raw_ref):
    left_total, coef_total = sums
    back_unit = force_unit * coef_total / left_total
    rho_bar = sc_ref[1:2, 0:1]
    phi_bar = sc_ref[2:3, 0:1]
    beta = jnp.sqrt(total(0)[0:1, TERMS : TERMS + 1] / left_total + tiny)
    scale = back_unit / beta
    lane = lax.broadcasted_iota(jnp.int32, (HALF, LANES), 1)
    wide = lax.broadcasted_iota(jnp.int32, (CHANNELS, LANES), 1)
    last = jnp.where(wide == CHANNELS, 1.0, 0.0)
    once = jnp.where(wide < CHANNELS, 1.0 / math.sqrt(CHANNELS), last) * scale
    twice = jnp.where(wide < CHANNELS, 2.0 / CHANNELS, last) * scale
    power = jnp.zeros((1, TERMS), jnp.float32)
    for z in range(SPECIES):
        at = slice(z * BLOCK, (z + 1) * BLOCK)
        packed = total(z)
        square = jnp.concatenate(
            [packed, jnp.zeros((LANES - HALF, LANES), jnp.float32)], axis=0
        )
        lower = jnp.where(lane < HALF, square.T[HALF:CHANNELS, :], turn(packed, -MOVE))
        back = jnp.concatenate([packed, lower], axis=0)
        v = (once * back)[:, :TERMS] - beta * v_ref[z]
        v_ref[z] = v
        power = power + row_sum(v * v)
        pair_ref[:, at] = twice * back - beta * pair_ref[:, at]
    alpha = jnp.sqrt(jnp.sum(power, axis=1, keepdims=True) / coef_total + tiny)
    rho = jnp.sqrt(rho_bar * rho_bar + beta * beta)
    cosine = rho_bar / rho
    sine = beta / rho
    theta = sine * alpha
    phi = cosine * phi_bar
    inverse = 1.0 / alpha
    for z in range(SPECIES):
        at = slice(z * BLOCK, (z + 1) * BLOCK)
        v = v_ref[z] * inverse
        v_ref[z] = v
        w = w_ref[z]
        x_ref[z] = x_ref[z] + (phi / rho) * w
        w_ref[z] = v - (theta / rho) * w
        pair_ref[:, at] = pair_ref[:, at] * inverse
    raw_ref[...] = raw_ref[...] / beta
    write_scalars(sc_ref, alpha, -cosine * alpha, sine * phi_bar)


def write_scalars(ref, alpha, rho_bar, phi_bar):
    row_id = lax.broadcasted_iota(jnp.int32, ref.shape, 0)
    ref[...] = jnp.where(row_id == 0, alpha, jnp.where(row_id == 1, rho_bar, phi_bar))


def sweep(own_count, alpha, left, pair_ref, psi_ref, delta_ref, near_ref, masked_ref, own_ref,
          raw_ref, out_ref, slope_ref, pull_ref, rhs_ref, lhs_ref):
    width = masked_ref.shape[1]
    unit = 2.0 / cutoff_sq
    slope_ref[...] = jnp.dot(
        pair_ref[...], masked_ref[...], precision=HIGHEST, preferred_element_type=jnp.float32
    )
    for tile in range(width // LANES):
        at = slice(tile * LANES, (tile + 1) * LANES)
        parts = [slope_ref[c * RADIAL : (c + 1) * RADIAL, at] for c in range(SPECIES)]
        for side in range(2):
            for o in range(WINDOW):
                kind = jnp.broadcast_to(near_ref[side, o : o + 1, at], (RADIAL, LANES))
                chosen = parts[0]
                for c in range(1, SPECIES):
                    chosen = jnp.where(kind == c, parts[c], chosen)
                pull_ref[side, o : o + 1, at] = row_sum(chosen * psi_ref[side, o, :, at])
    force = jnp.zeros((8, width), jnp.float32)
    for o in range(1, WINDOW + 1):
        pull = pull_ref[0, o - 1 : o, :] + turn(pull_ref[1, o - 1 : o, :], -o)
        term = (unit * pull) * delta_ref[o - 1]
        force = force + term - turn(term, o)
    raw = force_unit * force - alpha * left
    raw_ref[...] = raw
    for o in range(1, WINDOW + 1):
        project = unit * row_sum(delta_ref[o - 1] * (raw - turn(raw, -o)))
        pull_ref[0, o - 1 : o, :] = project
        pull_ref[1, o - 1 : o, :] = turn(project, o)
    for tile in range(own_count // LANES):
        at = slice(tile * LANES, (tile + 1) * LANES)
        behind = slice(own_count + tile * LANES, own_count + (tile + 1) * LANES)
        sums = [jnp.zeros((RADIAL, LANES), jnp.float32) for _ in range(SPECIES)]
        for side in range(2):
            for o in range(WINDOW):
                value = psi_ref[side, o, :, at] * pull_ref[side, o : o + 1, at]
                kind = jnp.broadcast_to(near_ref[side, o : o + 1, at], (RADIAL, LANES))
                for c in range(SPECIES):
                    sums[c] = sums[c] + jnp.where(kind == c, value, 0.0)
        for c in range(SPECIES):
            rhs_ref[c * RADIAL : (c + 1) * RADIAL, at] = sums[c]
        for z in range(SPECIES):
            own = own_ref[z : z + 1, at]
            for c in range(SPECIES):
                start = z * BLOCK + c * RADIAL
                lhs_ref[start : start + RADIAL, behind] = jnp.where(own > 0.5, sums[c], 0.0)
    cross = lax.dot_general(
        rhs_ref[...], lhs_ref[...], (((1,), (1,)), ((), ())),
        precision=HIGHEST, preferred_element_type=jnp.float32,
    )
    lane = lax.broadcasted_iota(jnp.int32, (HALF, LANES), 1)
    mine = raw[:, :own_count]
    square = jnp.sum(row_sum(mine * mine), axis=1, keepdims=True)
    for z in range(SPECIES):
        block = cross[:, z * BLOCK : (z + 1) * BLOCK]
        upper = jnp.where(lane == TERMS, square, block[:HALF])
        out_ref[z * HALF : (z + 1) * HALF, :] = jnp.where(
            lane < HALF + MOVE, upper, turn(block[HALF:], MOVE))


def kernel(n_snap, n_brick, own_count, sums,
           pos_in, species_in, words_in, left_in, v_in, w_in, x_in, sc_in,
           left_out, v_ref, w_ref, x_ref, sc_out,
           own_ref, ends, cells_ref, psi_ref, delta_ref, near_ref, masked_ref, kinds_ref, dens_ref,
           phi_ref, scaled_ref, pair_ref, sc_ref, raw_ref, slope_ref, pull_ref, rhs_ref, lhs_ref,
           part, slots, full, halo_send, halo_recv, send_a, recv_a, send_b, recv_b):
    count = n_snap * n_brick
    owners = min(count, ROWS // 8)
    stride = count // owners
    rows = ROWS // owners
    snap = lax.axis_index("snap")
    brick = lax.axis_index("brick")
    me = snap * n_brick + brick
    barrier = pltpu.get_barrier_semaphore()

    def device(p):
        return (p // n_brick, lax.rem(p, n_brick))

    def everyone(act):
        def body(k, carry):
            act(lax.rem(me + k, count))
            return carry
        lax.fori_loop(1, count, body, 0)

    def every_owner(act):
        if stride == 1:
            everyone(act)
        else:
            def body(k, carry):
                p = lax.rem(me // stride + k, owners) * stride

                @pl.when(p != me)
                def _():
                    act(p)
                return carry
            lax.fori_loop(0, owners, body, 0)

    def when_owner(yes, no):
        if stride == 1:
            yes()
        else:
            pl.when(lax.rem(me, stride) == 0)(yes)
            pl.when(lax.rem(me, stride) != 0)(no)

    everyone(lambda p: pl.semaphore_signal(
        barrier, inc=1, device_id=device(p), device_id_type=MESH))

    for k in range(3):
        own_ref[k : k + 1, :] = pos_in[k]
        own_ref[5 + k : 6 + k, :] = left_in[k]
    own_ref[3:4, :] = species_in[...].astype(jnp.float32)
    own_ref[4:5, :] = words_in[...].astype(jnp.float32)
    pl.semaphore_wait(barrier, count - 1)

    def shift(step, source, slot):
        return pltpu.make_async_remote_copy(
            src_ref=own_ref.at[:, pl.ds(source, LANES)], dst_ref=ends.at[slot],
            send_sem=halo_send.at[slot], recv_sem=halo_recv.at[slot],
            device_id=(snap, lax.rem(brick + step + n_brick, n_brick)), device_id_type=MESH,
        )

    to_left = shift(-1, 0, 0)
    to_right = shift(1, own_count - LANES, 1)
    has_left = brick > 0
    has_right = brick < n_brick - 1
    pl.when(has_left)(to_left.start)
    pl.when(has_right)(to_right.start)

    write_scalars(sc_ref, sc_in[0], sc_in[1], sc_in[2])
    rhs_ref[...] = jnp.zeros(rhs_ref.shape, jnp.float32)
    lhs_ref[...] = jnp.zeros(lhs_ref.shape, jnp.float32)
    fill = jnp.zeros((CHANNELS, LANES - TERMS), jnp.float32)
    wide = lax.broadcasted_iota(jnp.int32, (CHANNELS, LANES), 1)
    for z in range(SPECIES):
        v = v_in[z]
        v_ref[z] = v
        w_ref[z] = w_in[z]
        x_ref[z] = x_in[z]
        padded = jnp.concatenate([v, fill], axis=1)
        tall = jnp.concatenate([padded, jnp.zeros((LANES - CHANNELS, LANES), jnp.float32)], axis=0)
        pair = (padded + tall.T[:CHANNELS, :]) * (1.0 / math.sqrt(CHANNELS))
        pair_ref[:, z * BLOCK : (z + 1) * BLOCK] = jnp.where(wide < CHANNELS, pair, padded)

    @pl.when(has_left)
    def _():
        to_left.wait_send()
        to_right.wait_recv()

    @pl.when(has_right)
    def _():
        to_right.wait_send()
        to_left.wait_recv()

    zero = jnp.zeros((8, LANES), jnp.float32)

    @pl.when(jnp.logical_not(has_left))
    def _():
        ends[1] = zero

    @pl.when(jnp.logical_not(has_right))
    def _():
        ends[0] = zero

    cells_ref[:, :own_count] = own_ref[...]
    lane = lax.broadcasted_iota(jnp.int32, (8, LANES), 1)
    cells_ref[:, own_count:] = jnp.where(lane < HALO, ends[0], ends[1])
    prepare(cells_ref, psi_ref, delta_ref, near_ref, masked_ref, kinds_ref, dens_ref, phi_ref,
            scaled_ref)
    raw_ref[...] = jnp.zeros(raw_ref.shape, jnp.float32)
    raw_ref[0:3, :] = cells_ref[5:8, :]
    lhs_ref[:, :own_count] = masked_ref[:, :own_count]
    rhs_ref[:, own_count:] = dens_ref[:, :own_count]

    def chunk(ref, i, p):
        return ref.at[i, pl.ds(pl.multiple_of((p // stride) * rows, rows), rows), :]

    def reduce(i):
        def settle(ref, amount, sem):
            view = ref.at[i, pl.ds(0, amount)]
            pltpu.make_async_copy(view, view, sem.at[i]).wait()

        def send_part(p):
            pltpu.make_async_remote_copy(
                src_ref=chunk(part, i, p), dst_ref=slots.at[i, me], send_sem=send_a.at[i],
                recv_sem=recv_a.at[i], device_id=device(p), device_id_type=MESH,
            ).start()

        every_owner(send_part)

        def finish_owner():
            mine = pl.ds(pl.multiple_of((me // stride) * rows, rows), rows)
            slots[i, me] = part[i, mine, :]
            settle(slots, count - 1, recv_a)

            def add(p, total):
                return total + slots[i, p]
            full[i, mine, :] = lax.fori_loop(1, count, add, slots[i, 0], unroll=min(count - 1, 31))

            def send_sum(p):
                pltpu.make_async_remote_copy(
                    src_ref=chunk(full, i, me), dst_ref=chunk(full, i, me),
                    send_sem=send_b.at[i], recv_sem=recv_b.at[i], device_id=device(p),
                    device_id_type=MESH,
                ).start()

            everyone(send_sum)
            settle(full, (owners - 1) * rows, send_a)
            settle(full, (owners - 1) * rows, recv_b)
            settle(slots, count - 1, send_b)

        def finish_other():
            settle(full, owners * rows, send_a)
            settle(full, owners * rows, recv_b)

        when_owner(finish_owner, finish_other)

    def step(i, carry):
        sweep(own_count, sc_ref[0:1, 0:1], raw_ref[...], pair_ref, psi_ref, delta_ref, near_ref,
              masked_ref, kinds_ref, raw_ref, part.at[i], slope_ref, pull_ref, rhs_ref, lhs_ref)
        reduce(i)
        advance(lambda z: full[i, z * HALF : (z + 1) * HALF, :], sums, v_ref, w_ref, x_ref,
                pair_ref, sc_ref, raw_ref)
        return carry

    if ROWS > SPECIES * HALF:
        for i in range(ITERS):
            part[i, SPECIES * HALF :, :] = jnp.zeros((ROWS - SPECIES * HALF, LANES), jnp.float32)
    lax.fori_loop(0, ITERS, step, 0)
    for k in range(3):
        left_out[k] = raw_ref[k : k + 1, :own_count]
    at = lax.broadcasted_iota(jnp.int32, (1, 3), 1)
    sc_out[...] = jnp.where(
        at == 0, sc_ref[0:1, 0:1], jnp.where(at == 1, sc_ref[1:2, 0:1], sc_ref[2:3, 0:1]))


def shards(n_snap, n_brick, positions, species, atom_words, left_vector, right_vector, direction,
           solution_in, scalars):
    own_count = positions.shape[2]
    width = own_count + 2 * HALO
    coef_total = float(right_vector.size)
    left_total = float(3 * own_count * n_snap * n_brick * positions.shape[0])
    count = n_snap * n_brick
    owners = min(count, ROWS // 8)
    f32 = jnp.float32

    def shape(*dims):
        return jax.ShapeDtypeStruct(dims, f32)

    def room(*dims):
        return pltpu.VMEM(dims, f32)

    vmem = pl.BlockSpec(memory_space=pltpu.VMEM)
    smem = pl.BlockSpec(memory_space=pltpu.SMEM)
    coefs = shape(SPECIES, CHANNELS, TERMS)
    sem = pltpu.SemaphoreType.DMA
    left_next, v, w, x, sc = pl.pallas_call(
        functools.partial(kernel, n_snap, n_brick, own_count, (left_total, coef_total)),
        out_shape=[shape(3, 1, own_count), coefs, coefs, coefs, shape(1, 3)],
        in_specs=[vmem] * 7 + [smem], out_specs=[vmem] * 5,
        scratch_shapes=[
            room(8, own_count), room(2, 8, LANES), room(8, width), room(2, 16, RADIAL, width),
            room(16, 8, width), room(2, 16, width), room(SPECIES * BLOCK, width), room(8, width),
            room(CHANNELS, width), room(2, 16, RADIAL, width), room(16, width),
            room(CHANNELS, SPECIES * BLOCK), room(8, LANES), room(8, width),
            room(CHANNELS, width), room(2, 16, width), room(CHANNELS, 2 * own_count),
            room(SPECIES * BLOCK, 2 * own_count), room(ITERS, ROWS, LANES),
            room(ITERS, count, ROWS // owners, LANES), room(ITERS, ROWS, LANES),
            sem((2,)), sem((2,)), sem((ITERS,)), sem((ITERS,)), sem((ITERS,)), sem((ITERS,)),
        ],
        compiler_params=pltpu.CompilerParams(
            collective_id=0, has_side_effects=True, vmem_limit_bytes=40 * 2**20),
    )(
        jnp.swapaxes(positions, 0, 1), species, atom_words, jnp.swapaxes(left_vector, 0, 1),
        jnp.swapaxes(right_vector, 1, 2), jnp.swapaxes(direction, 1, 2),
        jnp.swapaxes(solution_in, 1, 2), scalars,
    )
    return (jnp.swapaxes(left_next, 0, 1), jnp.swapaxes(v, 1, 2), jnp.swapaxes(w, 1, 2),
            jnp.swapaxes(x, 1, 2), sc[0])


def solution(mesh):
    placed = (
        P("snap", None, "brick"), P("snap", "brick"), P("snap", "brick"),
        P("snap", None, "brick"), P(), P(), P(), P(),
    )
    return jax.shard_map(
        functools.partial(shards, mesh.shape["snap"], mesh.shape["brick"]),
        mesh=mesh, in_specs=placed,
        out_specs=(P("snap", None, "brick"), P(), P(), P(), P()), check_vma=False,
    )
```

time: 81.3 us -> 61 us (0.75)
  local copies, waits for them, and re-layouts: 14.4 us -> 6.61 us
  Pallas kernels: 59.5 us -> 53.4 us
  starting transfers between devices: 4.44 us -> 0 us
  other arithmetic: 1.61 us -> 0 us
    pallas_call x7 -> x1, Pallas kernels: 59.5 us -> 53.4 us  [shards(): pl.pallas_call(functools.partial(kernel, n_snap, n_brick, own_count, (lef...]
    unnamed x38 -> x21, local copies, waits for them, and re-layouts: 12.3 us -> 6.61 us
    ppermute x2 -> x0, starting transfers between devices: 4.44 us -> none  [the longest x1 3.16 us: shards(): lax.ppermute(own[:, -HALO:], 'brick', [(i, i + 1) for i in range(n_brick...]
    slice x4 -> x0, local copies, waits for them, and re-layouts: 1.86 us -> none  [the longest x1 1.04 us: shards(): right_vector[:, CHANNELS:, :]]
    convert_element_type x2 -> x0, other arithmetic: 1.37 us -> none  [the longest x1 0.69 us: shards(): species.astype(f32)]
  transfers between devices with their start and end apart: 2 -> 0, of which waited for: 0 -> 0; matrix products, arithmetic and copies ran while one was open for 2% -> 0% of each run, Pallas kernels for 0% -> 0%
where the time goes in v2:
time: 61 us; the launch traced here: 60.7 us
  Pallas kernels  53.4 us (88%)
  local copies, waits for them, and re-layouts  6.61 us (11%)
  between operations  0.69 us (1%)
    pallas_call x1, Pallas kernels, shards(): pl.pallas_call(functools.partial(kernel, n_snap, n_brick, own_count, (lef...  53.4 us
    unnamed x21, local copies, waits for them, and re-layouts  6.61 us

profile of v2, /device:TPU:0, one launch (start us, length us, event | category | flops | bytes accessed | tf_op | source)
XLA Modules:
  0.0 60.7 jit_solution(2078587710409067914)
XLA Ops:
  0.6 0.0 copy-start.6
  0.6 0.0 copy-start.4
  0.7 0.0 copy-start.3
  0.7 0.0 copy-start.5
  0.7 0.0 copy-start.7
  0.7 0.6 %copy-done.6 = s32[1,256]{1,0:T(1,128)S(1)} copy-done((s32[1,256]{1,0:T(1,128)S(1)}, s32[1,256]{1,0:T(1,128)}, u32[]{:S(2)}) %copy-start.6) | copy-done | bytes 1048
  1.3 0.0 copy-done.4
  1.3 0.0 copy-done.3
  1.4 0.0 copy-done.5
  1.4 0.0 copy-done.7
  1.4 0.0 copy-start
  1.4 0.9 %copy-done = f32[5,81,80]{1,2,0:T(8,128)S(1)} copy-done((f32[5,81,80]{1,2,0:T(8,128)S(1)}, f32[5,81,80]{1,2,0:T(8,128)}, u32[]{:S(2)}) %copy-start) | copy-done | bytes 129624
  2.3 0.0 copy-start.1
  2.3 0.9 %copy-done.1 = f32[5,81,80]{1,2,0:T(8,128)S(1)} copy-done((f32[5,81,80]{1,2,0:T(8,128)S(1)}, f32[5,81,80]{1,2,0:T(8,128)}, u32[]{:S(2)}) %copy-start.1) | copy-done | bytes 129624
  3.2 0.0 copy-start.2
  3.2 0.9 %copy-done.2 = f32[5,81,80]{1,2,0:T(8,128)S(1)} copy-done((f32[5,81,80]{1,2,0:T(8,128)S(1)}, f32[5,81,80]{1,2,0:T(8,128)}, u32[]{:S(2)}) %copy-start.2) | copy-done | bytes 129624
  4.2 53.4 %shard_map.119 = (f32[3,1,256]{2,1,0:T(1,128)S(1)}, f32[5,80,81]{2,1,0:T(8,128)S(1)}, f32[5,80,81]{2,1,0:T(8,128)S(1)}, f32[5,80,81]{2,1,0:T(8,128)S(1)}, f32[1,3]{1,0:T(1,128)S(1)}) custom-call(f32[3,1,256]{2,1,0:T(1,128)S(1)} %bitcast.16, s32[1,256]{1,0:T(1,128)S(1)} %copy-done.5, s32[1,256]{1,0:T(1,128)S(1)} %copy-done.6, f32[3,1,256]{2,1,0:T(1,128)S(1)} %bitcast.17, ...), custom_call_target="tpu_custom_call" | custom-call | tf_op jit(solution)/shard_map/pallas_call | solution.py:412
  57.6 0.6 copy.18
  58.2 0.7 %copy.19 = f32[5,81,80]{1,2,0:T(8,128)} copy(f32[5,81,80]{1,2,0:T(8,128)S(1)} %bitcast.12) | data formatting | bytes 259200
  58.9 0.7 %copy.20 = f32[5,81,80]{1,2,0:T(8,128)} copy(f32[5,81,80]{1,2,0:T(8,128)S(1)} %bitcast.11) | data formatting | bytes 259200
  59.5 0.7 %copy.21 = f32[5,81,80]{1,2,0:T(8,128)} copy(f32[5,81,80]{1,2,0:T(8,128)S(1)} %bitcast.10) | data formatting | bytes 259200
  60.2 0.5 copy.22
Async XLA Ops:
  0.6 0.7 %copy-start.6 = (s32[1,256]{1,0:T(1,128)S(1)}, s32[1,256]{1,0:T(1,128)}, u32[]{:S(2)}) copy-start(s32[1,256]{1,0:T(1,128)} %words_in.1) | copy-start | bytes 3076
  0.6 0.7 %copy-start.4 = (f32[1,3,256]{2,0,1:T(1,128)S(1)}, f32[1,3,256]{2,0,1:T(1,128)}, u32[]{:S(2)}) copy-start(f32[1,3,256]{2,0,1:T(1,128)} %param.11) | copy-start | bytes 9220
  0.7 0.7 %copy-start.3 = (f32[1,3,256]{2,0,1:T(1,128)S(1)}, f32[1,3,256]{2,0,1:T(1,128)}, u32[]{:S(2)}) copy-start(f32[1,3,256]{2,0,1:T(1,128)} %param.8) | copy-start | bytes 9220
  0.7 0.7 %copy-start.5 = (s32[1,256]{1,0:T(1,128)S(1)}, s32[1,256]{1,0:T(1,128)}, u32[]{:S(2)}) copy-start(s32[1,256]{1,0:T(1,128)} %species_in.1) | copy-start | bytes 3076
  0.7 0.7 %copy-start.7 = (f32[3]{0:T(128)S(1)}, f32[3]{0:T(128)}, u32[]{:S(2)}) copy-start(f32[3]{0:T(128)} %sc_in.1) | copy-start | bytes 40
  1.4 0.9 %copy-start = (f32[5,81,80]{1,2,0:T(8,128)S(1)}, f32[5,81,80]{1,2,0:T(8,128)}, u32[]{:S(2)}) copy-start(f32[5,81,80]{1,2,0:T(8,128)} %param.12) | copy-start | bytes 388804
  2.3 0.9 %copy-start.1 = (f32[5,81,80]{1,2,0:T(8,128)S(1)}, f32[5,81,80]{1,2,0:T(8,128)}, u32[]{:S(2)}) copy-start(f32[5,81,80]{1,2,0:T(8,128)} %param.13) | copy-start | bytes 388804
  3.2 0.9 %copy-start.2 = (f32[5,81,80]{1,2,0:T(8,128)S(1)}, f32[5,81,80]{1,2,0:T(8,128)}, u32[]{:S(2)}) copy-start(f32[5,81,80]{1,2,0:T(8,128)} %param.14) | copy-start | bytes 388804

commit v3 on v2

--- a/solution.py
+++ b/solution.py
@@ -20,6 +20,7 @@
 ROWS = 256
 LANES = 128
 HALO = 64
+INNER = 4
 
 cutoff_sq = 36.0
 spacing = 0.25
@@ -219,54 +220,58 @@
            left_out, v_ref, w_ref, x_ref, sc_out,
            own_ref, ends, cells_ref, psi_ref, delta_ref, near_ref, masked_ref, kinds_ref, dens_ref,
            phi_ref, scaled_ref, pair_ref, sc_ref, raw_ref, slope_ref, pull_ref, rhs_ref, lhs_ref,
-           part, slots, full, halo_send, halo_recv, send_a, recv_a, send_b, recv_b):
-    count = n_snap * n_brick
-    owners = min(count, ROWS // 8)
-    stride = count // owners
-    rows = ROWS // owners
+           part, slots, lines, full, halo_send, halo_recv, send_a, recv_a, send_b, recv_b, send_c,
+           recv_c, load):
+    inner = math.gcd(n_brick, INNER)
+    plane = n_snap * inner
+    depth = n_brick // inner
+    rows = ROWS // plane
     snap = lax.axis_index("snap")
     brick = lax.axis_index("brick")
-    me = snap * n_brick + brick
+    level = brick // inner
+    spot = snap * inner + lax.rem(brick, inner)
     barrier = pltpu.get_barrier_semaphore()
 
-    def device(p):
-        return (p // n_brick, lax.rem(p, n_brick))
-
-    def everyone(act):
-        def body(k, carry):
-            act(lax.rem(me + k, count))
-            return carry
-        lax.fori_loop(1, count, body, 0)
-
-    def every_owner(act):
-        if stride == 1:
-            everyone(act)
+    loads = [pltpu.make_async_copy(source, target, load.at[k]) for k, (source, target) in
+             enumerate(((v_in, v_ref), (w_in, w_ref), (x_in, x_ref)))]
+    for copy in loads:
+        copy.start()
+
+    def in_plane(q):
+        return (q // inner, level * inner + lax.rem(q, inner))
+
+    def in_line(q):
+        return (snap, q * inner + lax.rem(brick, inner))
+
+    def others(me, count, act):
+        if count <= 8:
+            for k in range(1, count):
+                act(lax.rem(me + k, count))
         else:
             def body(k, carry):
-                p = lax.rem(me // stride + k, owners) * stride
-
-                @pl.when(p != me)
-                def _():
-                    act(p)
+                act(lax.rem(me + k, count))
                 return carry
-            lax.fori_loop(0, owners, body, 0)
-
-    def when_owner(yes, no):
-        if stride == 1:
-            yes()
-        else:
-            pl.when(lax.rem(me, stride) == 0)(yes)
-            pl.when(lax.rem(me, stride) != 0)(no)
-
-    everyone(lambda p: pl.semaphore_signal(
-        barrier, inc=1, device_id=device(p), device_id_type=MESH))
+            lax.fori_loop(1, count, body, 0)
+
+    def greet(where):
+        pl.semaphore_signal(barrier, inc=1, device_id=where, device_id_type=MESH)
+
+    has_left = brick > 0
+    has_right = brick < n_brick - 1
+    cross_left = jnp.logical_and(has_left, lax.rem(brick, inner) == 0)
+    cross_right = jnp.logical_and(has_right, lax.rem(brick, inner) == inner - 1)
+    pl.when(cross_left)(lambda: greet((snap, brick - 1)))
+    pl.when(cross_right)(lambda: greet((snap, brick + 1)))
+    others(spot, plane, lambda q: greet(in_plane(q)))
+    others(level, depth, lambda q: greet(in_line(q)))
 
     for k in range(3):
         own_ref[k : k + 1, :] = pos_in[k]
         own_ref[5 + k : 6 + k, :] = left_in[k]
     own_ref[3:4, :] = species_in[...].astype(jnp.float32)
     own_ref[4:5, :] = words_in[...].astype(jnp.float32)
-    pl.semaphore_wait(barrier, count - 1)
+    pl.semaphore_wait(
+        barrier, plane + depth - 2 + jnp.where(cross_left, 1, 0) + jnp.where(cross_right, 1, 0))
 
     def shift(step, source, slot):
         return pltpu.make_async_remote_copy(
@@ -277,8 +282,6 @@
 
     to_left = shift(-1, 0, 0)
     to_right = shift(1, own_count - LANES, 1)
-    has_left = brick > 0
-    has_right = brick < n_brick - 1
     pl.when(has_left)(to_left.start)
     pl.when(has_right)(to_right.start)
 
@@ -287,11 +290,9 @@
     lhs_ref[...] = jnp.zeros(lhs_ref.shape, jnp.float32)
     fill = jnp.zeros((CHANNELS, LANES - TERMS), jnp.float32)
     wide = lax.broadcasted_iota(jnp.int32, (CHANNELS, LANES), 1)
+    loads[0].wait()
     for z in range(SPECIES):
-        v = v_in[z]
-        v_ref[z] = v
-        w_ref[z] = w_in[z]
-        x_ref[z] = x_in[z]
+        v = v_ref[z]
         padded = jnp.concatenate([v, fill], axis=1)
         tall = jnp.concatenate([padded, jnp.zeros((LANES - CHANNELS, LANES), jnp.float32)], axis=0)
         pair = (padded + tall.T[:CHANNELS, :]) * (1.0 / math.sqrt(CHANNELS))
@@ -327,48 +328,41 @@
     lhs_ref[:, :own_count] = masked_ref[:, :own_count]
     rhs_ref[:, own_count:] = dens_ref[:, :own_count]
 
-    def chunk(ref, i, p):
-        return ref.at[i, pl.ds(pl.multiple_of((p // stride) * rows, rows), rows), :]
+    def chunk(q):
+        return pl.ds(pl.multiple_of(q * rows, rows), rows)
+
+    def settle(ref, i, amount, sem):
+        view = ref.at[i, pl.ds(0, amount)]
+        pltpu.make_async_copy(view, view, sem.at[i]).wait()
+
+    def send(source, target, sent, got, i, where):
+        pltpu.make_async_remote_copy(
+            src_ref=source, dst_ref=target, send_sem=sent.at[i], recv_sem=got.at[i],
+            device_id=where, device_id_type=MESH,
+        ).start()
+
+    def add_up(ref, i, count):
+        total = ref[i, 0]
+        for q in range(1, count):
+            total = total + ref[i, q]
+        return total
 
     def reduce(i):
-        def settle(ref, amount, sem):
-            view = ref.at[i, pl.ds(0, amount)]
-            pltpu.make_async_copy(view, view, sem.at[i]).wait()
-
-        def send_part(p):
-            pltpu.make_async_remote_copy(
-                src_ref=chunk(part, i, p), dst_ref=slots.at[i, me], send_sem=send_a.at[i],
-                recv_sem=recv_a.at[i], device_id=device(p), device_id_type=MESH,
-            ).start()
-
-        every_owner(send_part)
-
-        def finish_owner():
-            mine = pl.ds(pl.multiple_of((me // stride) * rows, rows), rows)
-            slots[i, me] = part[i, mine, :]
-            settle(slots, count - 1, recv_a)
-
-            def add(p, total):
-                return total + slots[i, p]
-            full[i, mine, :] = lax.fori_loop(1, count, add, slots[i, 0], unroll=min(count - 1, 31))
-
-            def send_sum(p):
-                pltpu.make_async_remote_copy(
-                    src_ref=chunk(full, i, me), dst_ref=chunk(full, i, me),
-                    send_sem=send_b.at[i], recv_sem=recv_b.at[i], device_id=device(p),
-                    device_id_type=MESH,
-                ).start()
-
-            everyone(send_sum)
-            settle(full, (owners - 1) * rows, send_a)
-            settle(full, (owners - 1) * rows, recv_b)
-            settle(slots, count - 1, send_b)
-
-        def finish_other():
-            settle(full, owners * rows, send_a)
-            settle(full, owners * rows, recv_b)
-
-        when_owner(finish_owner, finish_other)
+        others(spot, plane, lambda q: send(
+            part.at[i, chunk(q)], slots.at[i, spot], send_a, recv_a, i, in_plane(q)))
+        slots[i, spot] = part[i, chunk(spot), :]
+        settle(slots, i, plane - 1, recv_a)
+        lines[i, level] = add_up(slots, i, plane)
+        others(level, depth, lambda q: send(
+            lines.at[i, level], lines.at[i, level], send_b, recv_b, i, in_line(q)))
+        settle(lines, i, depth - 1, recv_b)
+        full[i, chunk(spot), :] = add_up(lines, i, depth)
+        others(spot, plane, lambda q: send(
+            full.at[i, chunk(spot)], full.at[i, chunk(spot)], send_c, recv_c, i, in_plane(q)))
+        settle(slots, i, plane - 1, send_a)
+        settle(lines, i, depth - 1, send_b)
+        settle(slots, i, plane - 1, recv_c)
+        settle(slots, i, plane - 1, send_c)
 
     def step(i, carry):
         sweep(own_count, sc_ref[0:1, 0:1], raw_ref[...], pair_ref, psi_ref, delta_ref, near_ref,
@@ -381,6 +375,8 @@
     if ROWS > SPECIES * HALF:
         for i in range(ITERS):
             part[i, SPECIES * HALF :, :] = jnp.zeros((ROWS - SPECIES * HALF, LANES), jnp.float32)
+    loads[1].wait()
+    loads[2].wait()
     lax.fori_loop(0, ITERS, step, 0)
     for k in range(3):
         left_out[k] = raw_ref[k : k + 1, :own_count]
@@ -389,14 +385,22 @@
         at == 0, sc_ref[0:1, 0:1], jnp.where(at == 1, sc_ref[1:2, 0:1], sc_ref[2:3, 0:1]))
 
 
+def store_kernel(*refs):
+    copies = [pltpu.make_async_copy(refs[k], refs[5 + k], refs[10].at[k]) for k in range(5)]
+    for copy in copies:
+        copy.start()
+    for copy in copies:
+        copy.wait()
+
+
 def shards(n_snap, n_brick, positions, species, atom_words, left_vector, right_vector, direction,
            solution_in, scalars):
     own_count = positions.shape[2]
     width = own_count + 2 * HALO
     coef_total = float(right_vector.size)
     left_total = float(3 * own_count * n_snap * n_brick * positions.shape[0])
-    count = n_snap * n_brick
-    owners = min(count, ROWS // 8)
+    inner = math.gcd(n_brick, INNER)
+    plane = n_snap * inner
     f32 = jnp.float32
 
     def shape(*dims):
@@ -407,12 +411,14 @@
 
     vmem = pl.BlockSpec(memory_space=pltpu.VMEM)
     smem = pl.BlockSpec(memory_space=pltpu.SMEM)
+    hbm = pl.BlockSpec(memory_space=pltpu.HBM)
     coefs = shape(SPECIES, CHANNELS, TERMS)
     sem = pltpu.SemaphoreType.DMA
-    left_next, v, w, x, sc = pl.pallas_call(
+    shapes = [shape(3, 1, own_count), coefs, coefs, coefs, shape(1, 3)]
+    results = pl.pallas_call(
         functools.partial(kernel, n_snap, n_brick, own_count, (left_total, coef_total)),
-        out_shape=[shape(3, 1, own_count), coefs, coefs, coefs, shape(1, 3)],
-        in_specs=[vmem] * 7 + [smem], out_specs=[vmem] * 5,
+        out_shape=shapes,
+        in_specs=[vmem] * 4 + [hbm] * 3 + [smem], out_specs=[vmem] * 5,
         scratch_shapes=[
             room(8, own_count), room(2, 8, LANES), room(8, width), room(2, 16, RADIAL, width),
             room(16, 8, width), room(2, 16, width), room(SPECIES * BLOCK, width), room(8, width),
@@ -420,16 +426,22 @@
             room(CHANNELS, SPECIES * BLOCK), room(8, LANES), room(8, width),
             room(CHANNELS, width), room(2, 16, width), room(CHANNELS, 2 * own_count),
             room(SPECIES * BLOCK, 2 * own_count), room(ITERS, ROWS, LANES),
-            room(ITERS, count, ROWS // owners, LANES), room(ITERS, ROWS, LANES),
-            sem((2,)), sem((2,)), sem((ITERS,)), sem((ITERS,)), sem((ITERS,)), sem((ITERS,)),
+            room(ITERS, plane, ROWS // plane, LANES),
+            room(ITERS, n_brick // inner, ROWS // plane, LANES), room(ITERS, ROWS, LANES),
+            sem((2,)), sem((2,)), *[sem((ITERS,)) for _ in range(6)], sem((3,)),
         ],
         compiler_params=pltpu.CompilerParams(
-            collective_id=0, has_side_effects=True, vmem_limit_bytes=40 * 2**20),
+            collective_id=0, has_side_effects=True, vmem_limit_bytes=62 * 2**20),
     )(
         jnp.swapaxes(positions, 0, 1), species, atom_words, jnp.swapaxes(left_vector, 0, 1),
         jnp.swapaxes(right_vector, 1, 2), jnp.swapaxes(direction, 1, 2),
         jnp.swapaxes(solution_in, 1, 2), scalars,
     )
+    left_next, v, w, x, sc = pl.pallas_call(
+        store_kernel, out_shape=shapes, in_specs=[hbm] * 5, out_specs=[hbm] * 5,
+        scratch_shapes=[sem((5,))],
+        compiler_params=pltpu.CompilerParams(vmem_limit_bytes=62 * 2**20),
+    )(*results)
     return (jnp.swapaxes(left_next, 0, 1), jnp.swapaxes(v, 1, 2), jnp.swapaxes(w, 1, 2),
             jnp.swapaxes(x, 1, 2), sc[0])
 

time: 61 us -> 73 us (1.20)
  Pallas kernels: 53.4 us -> 72.2 us
  local copies, waits for them, and re-layouts: 6.61 us -> 0 us
    pallas_call x0 -> x1, Pallas kernels: none -> 19.9 us  [shards(): pl.pallas_call(store_kernel, out_shape=shapes, in_specs=[hbm] * 5, out_sp...]
    unnamed x21 -> x0, local copies, waits for them, and re-layouts: 6.61 us -> none
    pallas_call x1, Pallas kernels: 53.4 us -> 52.3 us  [shards(): pl.pallas_call(functools.partial(kernel, n_snap, n_brick, own_count, (lef...]
where the time goes in v3:
time: 73 us; the launch traced here: 72.8 us
  Pallas kernels  72.2 us (99%)
    pallas_call x1, Pallas kernels, shards(): pl.pallas_call(functools.partial(kernel, n_snap, n_brick, own_count, (lef...  52.3 us
    pallas_call x1, Pallas kernels, shards(): pl.pallas_call(store_kernel, out_shape=shapes, in_specs=[hbm] * 5, out_sp...  19.9 us

profile of v3, /device:TPU:0, one launch (start us, length us, event | category | flops | bytes accessed | tf_op | source)
XLA Modules:
  0.0 72.8 jit_solution(2653935019260695429)
XLA Ops:
  0.6 52.3 %shard_map.119 = (f32[3,1,256]{2,1,0:T(1,128)}, f32[5,80,81]{2,1,0:T(8,128)}, f32[5,80,81]{2,1,0:T(8,128)}, f32[5,80,81]{2,1,0:T(8,128)}, f32[1,3]{1,0:T(1,128)}) custom-call(f32[3,1,256]{2,1,0:T(1,128)} %bitcast.13, s32[1,256]{1,0:T(1,128)} %species_in.1, s32[1,256]{1,0:T(1,128)} %words_in.1, f32[3,1,256]{2,1,0:T(1,128)} %bitcast.14, ...), custom_call_target="tpu_custom_call" | custom-call | tf_op jit(solution)/shard_map/pallas_call | solution.py:418
  52.9 19.9 %shard_map.120 = (f32[3,1,256]{2,1,0:T(1,128)}, f32[5,80,81]{2,1,0:T(8,128)}, f32[5,80,81]{2,1,0:T(8,128)}, f32[5,80,81]{2,1,0:T(8,128)}, f32[1,3]{1,0:T(1,128)}) custom-call(f32[3,1,256]{2,1,0:T(1,128)} %get-tuple-element.15.refs_0_, f32[5,80,81]{2,1,0:T(8,128)} %get-tuple-element.16.refs_1_, f32[5,80,81]{2,1,0:T(8,128)} %get-tuple-element.17.refs_2_, ...), custom_call_target="tpu_custom_call" | custom-call | tf_op jit(solution)/shard_map/pallas_call | solution.py:440

commit v4 on v3

--- a/solution.py
+++ b/solution.py
@@ -26,7 +26,6 @@
 spacing = 0.25
 force_unit = 0.015625
 tiny = 1e-06
-HIGHEST = lax.Precision.HIGHEST
 MESH = pl.DeviceIdType.MESH
 
 
@@ -37,6 +36,19 @@
 
 def row_sum(x):
     return jnp.sum(x, axis=0, keepdims=True)
+
+
+def product(x, y, dims):
+    def halves(a):
+        high = a.astype(jnp.bfloat16)
+        return high, (a - high.astype(jnp.float32)).astype(jnp.bfloat16)
+
+    def dot(a, b):
+        return lax.dot_general(a, b, (dims, ((), ())), preferred_element_type=jnp.float32)
+
+    x_high, x_low = halves(x)
+    y_high, y_low = halves(y)
+    return dot(x_high, y_high) + (dot(x_high, y_low) + dot(x_low, y_high))
 
 
 def prepare(cells_ref, psi_ref, delta_ref, near_ref, masked_ref, own_ref, dens_ref, phi_ref,
@@ -160,9 +172,7 @@
           raw_ref, out_ref, slope_ref, pull_ref, rhs_ref, lhs_ref):
     width = masked_ref.shape[1]
     unit = 2.0 / cutoff_sq
-    slope_ref[...] = jnp.dot(
-        pair_ref[...], masked_ref[...], precision=HIGHEST, preferred_element_type=jnp.float32
-    )
+    slope_ref[...] = product(pair_ref[...], masked_ref[...], ((1,), (0,)))
     for tile in range(width // LANES):
         at = slice(tile * LANES, (tile + 1) * LANES)
         parts = [slope_ref[c * RADIAL : (c + 1) * RADIAL, at] for c in range(SPECIES)]
@@ -201,10 +211,7 @@
             for c in range(SPECIES):
                 start = z * BLOCK + c * RADIAL
                 lhs_ref[start : start + RADIAL, behind] = jnp.where(own > 0.5, sums[c], 0.0)
-    cross = lax.dot_general(
-        rhs_ref[...], lhs_ref[...], (((1,), (1,)), ((), ())),
-        precision=HIGHEST, preferred_element_type=jnp.float32,
-    )
+    cross = product(rhs_ref[...], lhs_ref[...], ((1,), (1,)))
     lane = lax.broadcasted_iota(jnp.int32, (HALF, LANES), 1)
     mine = raw[:, :own_count]
     square = jnp.sum(row_sum(mine * mine), axis=1, keepdims=True)
@@ -386,10 +393,14 @@
 
 
 def store_kernel(*refs):
-    copies = [pltpu.make_async_copy(refs[k], refs[5 + k], refs[10].at[k]) for k in range(5)]
-    for copy in copies:
+    loads = [pltpu.make_async_copy(refs[k], refs[10 + k], refs[15].at[k]) for k in range(5)]
+    stores = [pltpu.make_async_copy(refs[10 + k], refs[5 + k], refs[16].at[k]) for k in range(5)]
+    for copy in loads:
         copy.start()
-    for copy in copies:
+    for load, store in zip(loads, stores):
+        load.wait()
+        store.start()
+    for copy in stores:
         copy.wait()
 
 
@@ -439,7 +450,7 @@
     )
     left_next, v, w, x, sc = pl.pallas_call(
         store_kernel, out_shape=shapes, in_specs=[hbm] * 5, out_specs=[hbm] * 5,
-        scratch_shapes=[sem((5,))],
+        scratch_shapes=[room(*one.shape) for one in shapes] + [sem((5,)), sem((5,))],
         compiler_params=pltpu.CompilerParams(vmem_limit_bytes=62 * 2**20),
     )(*results)
     return (jnp.swapaxes(left_next, 0, 1), jnp.swapaxes(v, 1, 2), jnp.swapaxes(w, 1, 2),

time: 73 us -> 52.2 us (0.72)
  Pallas kernels: 72.2 us -> 51.3 us
    pallas_call x1, Pallas kernels: 19.9 us -> 1.9 us  [shards(): pl.pallas_call(store_kernel, out_shape=shapes, in_specs=[hbm] * 5, out_sp...]
    pallas_call x1, Pallas kernels: 52.3 us -> 49.4 us  [shards(): pl.pallas_call(functools.partial(kernel, n_snap, n_brick, own_count, (lef...]
where the time goes in v4:
time: 52.2 us; the launch traced here: 52 us
  Pallas kernels  51.3 us (98%)
  between operations  0.64 us (1%)
    pallas_call x1, Pallas kernels, shards(): pl.pallas_call(functools.partial(kernel, n_snap, n_brick, own_count, (lef...  49.4 us
    pallas_call x1, Pallas kernels, shards(): pl.pallas_call(store_kernel, out_shape=shapes, in_specs=[hbm] * 5, out_sp...  1.9 us

profile of v4, /device:TPU:0, one launch (start us, length us, event | category | flops | bytes accessed | tf_op | source)
XLA Modules:
  0.0 52.0 jit_solution(15211909784404999153)
XLA Ops:
  0.6 49.4 %shard_map.119 = (f32[3,1,256]{2,1,0:T(1,128)}, f32[5,80,81]{2,1,0:T(8,128)}, f32[5,80,81]{2,1,0:T(8,128)}, f32[5,80,81]{2,1,0:T(8,128)}, f32[1,3]{1,0:T(1,128)}) custom-call(f32[3,1,256]{2,1,0:T(1,128)} %bitcast.13, s32[1,256]{1,0:T(1,128)} %species_in.1, s32[1,256]{1,0:T(1,128)} %words_in.1, f32[3,1,256]{2,1,0:T(1,128)} %bitcast.14, ...), custom_call_target="tpu_custom_call" | custom-call | tf_op jit(solution)/shard_map/pallas_call | solution.py:429
  50.1 1.9 %shard_map.120 = (f32[3,1,256]{2,1,0:T(1,128)}, f32[5,80,81]{2,1,0:T(8,128)}, f32[5,80,81]{2,1,0:T(8,128)}, f32[5,80,81]{2,1,0:T(8,128)}, f32[1,3]{1,0:T(1,128)}) custom-call(f32[3,1,256]{2,1,0:T(1,128)} %get-tuple-element.15.refs_0_, f32[5,80,81]{2,1,0:T(8,128)} %get-tuple-element.16.refs_1_, f32[5,80,81]{2,1,0:T(8,128)} %get-tuple-element.17.refs_2_, ...), custom_call_target="tpu_custom_call" | custom-call | tf_op jit(solution)/shard_map/pallas_call | solution.py:451
